TPU v7x, 256 devices: a whole 4x4x8 slice. The times are simulated.
256 devices in a mesh: gx: 8 (over z), gy: 32 (over y, x, core).
Axes of the slice: x: 4, y: 4, z: 8, core: 2. Of those that a mesh axis runs over, the one named last changes fastest.
Arguments:
- adjoint_rhs: float32 [2, 3, 8, 2048, 128], P(None, None, 'gx', 'gy'), may hold values from -6 to 6
- block_inverse: float32 [3, 3, 8, 2048, 128], P(None, None, 'gx', 'gy'), may hold values from -0.3 to 1.3, as said below
- x_couplings: float32 [2, 3, 8, 2048, 128], P(None, None, 'gx', 'gy'), may hold values from -0.8 to -0.3
- y_couplings: float32 [2, 3, 8, 2048, 128], P(None, None, 'gx', 'gy'), may hold values from -0.3 to -0.05
- perf_cell: int32 [16384], P(('gx', 'gy')), may hold values from 0 to 8191
- perf_well: int32 [16384], P(('gx', 'gy')), may hold values from 0 to 1023
- perf_weight: float32 [16384], P(('gx', 'gy')), may hold values from 0.5 to 2
- well_adjoint: float32 [3, 1024], P(None, ('gx', 'gy')), may hold values from -6 to 6
Outputs:
- precond: float32 [2, 3, 8, 2048, 128], P(None, None, 'gx', 'gy')
- well_update: float32 [3, 1024], P(None, ('gx', 'gy'))
Inputs may be any that keep to these rules, and one draw needn't show every extreme that they name: `perf_cell`: local cell index within the owning device's block. `block_inverse`: diagonal entries are at least 0.5, off-diagonal ones at most 0.3 in magnitude.
All inputs are finite; a program needn't handle non-finite values.
Results may differ from a plain program's by a relative error of at most 0.00017.
Values sent between devices are 32-bit elements; how exact they have to be, the bound alone decides.
No kernel may reach another device: no remote copies, remote signals or barrier semaphores. Data moves between devices by JAX's collectives and lax.ppermute only.
A program may use at most 64 MiB of HBM per device.

v0:
```python
import jax
import jax.numpy as jnp
from jax import lax
from jax.sharding import PartitionSpec as P


def with_halo(shard, sides, width):
    for axis, dim in sides:
        peers, length = (lax.axis_size(axis), shard.shape[dim])
        up = [(i, (i + 1) % peers) for i in range(peers - 1)]
        down = [(j, i) for i, j in up]
        last = lax.slice_in_dim(shard, length - width, length, axis=dim)
        first = lax.slice_in_dim(shard, 0, width, axis=dim)
        before = lax.ppermute(last, axis, up)
        after = lax.ppermute(first, axis, down)
        shard = jnp.concatenate([before, shard, after], axis=dim)
    return shard


def passed_along(block, axis, distance):
    devices = range(lax.axis_size(axis))
    route = [(i - distance, i) for i in devices if i - distance in devices]
    return lax.ppermute(block, axis, route)


def apply_inverse(inverse, values):
    return (
        inverse[:, 0] * values[None, 0]
        + inverse[:, 1] * values[None, 1]
        + inverse[:, 2] * values[None, 2]
    )


def couple(values, padded, inverse, lower, upper):
    return apply_inverse(inverse, values - lower * padded[:, :, :-2] - upper * padded[:, :, 2:])


def plane_solve(values, inverse, lower, upper):
    weighted = apply_inverse(inverse, values)
    padded = with_halo(weighted, (("gy", 2),), 1)
    return couple(values, padded, inverse, lower, upper)


def march_forward(sources, block_inverse, x_low, lower, upper, inflow):
    planes = sources.shape[2]

    def step(plane, state):
        result, previous = state
        inverse = lax.dynamic_index_in_dim(block_inverse, plane, 2, True)
        low = lax.dynamic_index_in_dim(x_low, plane, 1, True)
        ylo = lax.dynamic_index_in_dim(lower, plane, 1, True)
        yup = lax.dynamic_index_in_dim(upper, plane, 1, True)
        source = lax.dynamic_index_in_dim(sources, plane, 2, False)
        current = plane_solve(source - low * previous, inverse, ylo, yup)
        result = lax.dynamic_update_index_in_dim(result, current, plane, 2)
        return (result, current)

    result, _ = lax.fori_loop(0, planes, step, (jnp.zeros_like(sources), inflow))
    return result


def march_backward(forward_planes, block_inverse, x_up, lower, upper, outflow):
    planes = forward_planes.shape[2]

    def step(count, state):
        result, following = state
        plane = planes - 1 - count
        inverse = lax.dynamic_index_in_dim(block_inverse, plane, 2, True)
        high = lax.dynamic_index_in_dim(x_up, plane, 1, True)
        ylo = lax.dynamic_index_in_dim(lower, plane, 1, True)
        yup = lax.dynamic_index_in_dim(upper, plane, 1, True)
        current_q = lax.dynamic_index_in_dim(forward_planes, plane, 2, False)
        current = current_q - plane_solve(high * following, inverse, ylo, yup)
        result = lax.dynamic_update_index_in_dim(result, current, plane, 2)
        return (result, current)

    result, _ = lax.fori_loop(0, planes, step, (jnp.zeros_like(forward_planes), outflow))
    return result


def precondition(rhs_cells, block_inverse, x_couplings, y_couplings):
    chain_size = lax.axis_size("gx")
    lower = y_couplings[0]
    upper = y_couplings[1]
    boundary_shape = (
        rhs_cells.shape[0],
        rhs_cells.shape[1],
        rhs_cells.shape[3],
        rhs_cells.shape[4],
    )
    inflow = jnp.zeros(boundary_shape, jnp.float32)
    forward_planes = rhs_cells
    for turn in range(chain_size):
        forward_planes = march_forward(
            rhs_cells, block_inverse, x_couplings[0], lower, upper, inflow
        )
        if turn + 1 < chain_size:
            inflow = passed_along(forward_planes[:, :, -1], "gx", 1)
    outflow = jnp.zeros(boundary_shape, jnp.float32)
    result = forward_planes
    for turn in range(chain_size):
        result = march_backward(
            forward_planes, block_inverse, x_couplings[1], lower, upper, outflow
        )
        if turn + 1 < chain_size:
            outflow = passed_along(result[:, :, 0], "gx", -1)
    return result


def both_applications(rhs_cells, block_inverse, x_couplings, y_couplings):
    first = precondition(rhs_cells[:, 0:1], block_inverse, x_couplings, y_couplings)
    second = precondition(rhs_cells[:, 1:2], block_inverse, x_couplings, y_couplings)
    return jnp.concatenate([first, second], axis=1)


def per_device(
    adjoint_rhs,
    block_inverse,
    x_couplings,
    y_couplings,
    perf_cell,
    perf_well,
    perf_weight,
    well_adjoint,
):
    all_wells = lax.all_gather(well_adjoint, ("gx", "gy"), axis=1, tiled=True)
    well_count = all_wells.shape[1]
    selector = (perf_well[:, None] == jnp.arange(well_count, dtype=jnp.int32)[None, :]).astype(
        jnp.float32
    )
    picked = jnp.dot(all_wells, selector.T, precision=lax.Precision.HIGHEST)
    terms = picked * perf_weight[None]
    comps = adjoint_rhs.shape[1]
    block_shape = adjoint_rhs.shape[2:]
    planes = block_shape[0]
    lines = block_shape[1]
    depth_cells = block_shape[2]
    cells = planes * lines * depth_cells
    source = jnp.zeros((comps, cells), jnp.float32).at[:, perf_cell].add(terms)
    source = source.reshape((comps,) + block_shape)
    rhs_cells = jnp.moveaxis(adjoint_rhs + source[None], 0, 1)
    solved = both_applications(rhs_cells, block_inverse, x_couplings, y_couplings)
    precond = jnp.moveaxis(solved, 1, 0)
    second_flat = precond[1].reshape(comps, cells)
    values = jnp.take(second_flat, perf_cell, axis=1) * perf_weight[None]
    local_sums = jnp.dot(values, selector, precision=lax.Precision.HIGHEST)
    well_update = lax.psum_scatter(local_sums, ("gx", "gy"), scatter_dimension=1, tiled=True)
    return (precond, well_update)


def solution(mesh):
    placed = (
        P(None, None, "gx", "gy", None),
        P(None, None, "gx", "gy", None),
        P(None, None, "gx", "gy", None),
        P(None, None, "gx", "gy", None),
        P(("gx", "gy")),
        P(("gx", "gy")),
        P(("gx", "gy")),
        P(None, ("gx", "gy")),
    )
    return jax.shard_map(
        per_device,
        mesh=mesh,
        in_specs=placed,
        out_specs=(P(None, None, "gx", "gy", None), P(None, ("gx", "gy"))),
        check_vma=False,
    )
```

profile of v0, /device:TPU:1, one launch (start us, length us, event | category | flops | bytes accessed | tf_op | source)
XLA Modules:
  0.0 626.7 jit_solution(9678886690940815121)
XLA Ops:
  2.1 73.0 %all-gather = f32[256,4,3]{2,1,0:T(4,128)S(1)} all-gather(f32[1,4,3]{2,1,0:T(4,128)S(1)} %bitcast.1524), channel_id=1, replica_groups=mesh['gx'=8,'gy'=32] {'gx','gy'}, dimensions={0}, use_global_device_ids=true | all-gather | bytes 12336 | tf_op jit(solution)/shard_map/all_gather | solution.py:126
  134.4 4.8 collective-permute-start.12
  174.7 7.2 %collective-permute-done.47 = f32[3,1,1,128]{3,2,0,1:T(1,128)S(1)} collective-permute-done((f32[3,1,1,128]{3,2,0,1:T(1,128)S(1)}, f32[3,1,1,128]{3,2,0,1:T(1,128)S(1)}, u32[]{:S(2)}, u32[]{:S(2)}) %collective-permute-start.47) | collective-permute-done | bytes 1568 | tf_op jit(solution)/shard_map/while/body/eval_jaxpr/ppermute | solution.py:15
  182.1 5.0 collective-permute-start.20
  187.1 5.1 collective-permute-start.48
  193.9 5.6 collective-permute-start.49
  204.5 4.9 collective-permute-start.51
  211.2 5.4 collective-permute-start.52
  221.6 4.9 collective-permute-start.54
  228.3 5.4 collective-permute-start.55
  287.1 5.2 collective-permute-start.66
  299.6 5.0 collective-permute-start.21
  348.4 6.1 collective-permute-start.29
  363.8 5.4 collective-permute-start.73
  372.5 5.1 collective-permute-done.74
  378.5 7.9 %collective-permute-start.32 = (f32[3,1,1,128]{3,2,0,1:T(1,128)S(1)}, f32[3,1,1,128]{3,2,0,1:T(1,128)S(1)}, u32[]{:S(2)}, u32[]{:S(2)}) collective-permute-start(f32[3,1,1,128]{3,2,0,1:T(1,128)S(1)} %get-tuple-element.742), channel_id=1, source_target_pairs={{0,1},{1,2},{2,3},{3,4},{4,5},{5,6},{6,7},{7,8},{8,9},{9,10},{10,1... | collective-permute-start | bytes 4616 | tf_op jit(solution)/shard_map/while/body/eval_jaxpr/ppermute | solution.py:14
  422.0 5.0 collective-permute-start.79
  449.3 4.8 collective-permute-start.82
  463.0 6.6 %collective-permute-start.41 = (f32[3,1,1,128]{3,2,0,1:T(1,128)S(1)}, f32[3,1,1,128]{3,2,0,1:T(1,128)S(1)}, u32[]{:S(2)}, u32[]{:S(2)}) collective-permute-start(f32[3,1,1,128]{3,2,0,1:T(1,128)S(1)} %get-tuple-element.691), channel_id=1, source_target_pairs={{0,1},{1,2},{2,3},{3,4},{4,5},{5,6},{6,7},{7,8},{8,9},{9,10},{10,1... | collective-permute-start | bytes 4616 | tf_op jit(solution)/shard_map/while/body/eval_jaxpr/ppermute | solution.py:14
  478.6 6.6 %collective-permute-start.85 = (f32[3,1,1,128]{3,2,0,1:T(1,128)S(1)}, f32[3,1,1,128]{3,2,0,1:T(1,128)S(1)}, u32[]{:S(2)}, u32[]{:S(2)}) collective-permute-start(f32[3,1,1,128]{3,2,0,1:T(1,128)S(1)} %get-tuple-element.937), channel_id=1, source_target_pairs={{0,1},{1,2},{2,3},{3,4},{4,5},{5,6},{6,7},{7,8},{8,9},{9,10},{10,1... | collective-permute-start | bytes 4616 | tf_op jit(solution)/shard_map/while/body/eval_jaxpr/ppermute | solution.py:14
  495.4 6.6 %collective-permute-start.44 = (f32[3,1,1,128]{3,2,0,1:T(1,128)S(1)}, f32[3,1,1,128]{3,2,0,1:T(1,128)S(1)}, u32[]{:S(2)}, u32[]{:S(2)}) collective-permute-start(f32[3,1,1,128]{3,2,0,1:T(1,128)S(1)} %get-tuple-element.674), channel_id=1, source_target_pairs={{0,1},{1,2},{2,3},{3,4},{4,5},{5,6},{6,7},{7,8},{8,9},{9,10},{10,1... | collective-permute-start | bytes 4616 | tf_op jit(solution)/shard_map/while/body/eval_jaxpr/ppermute | solution.py:14
  504.1 6.0 collective-permute-start.88
  512.1 5.9 collective-permute-done.89
  524.0 102.0 %all-reduce = f32[3,1024]{1,0:T(4,128)S(1)} all-reduce(f32[3,1024]{1,0:T(4,128)S(1)} %fusion.2), channel_id=2, replica_groups=mesh['gx'=8,'gy'=32] {'gx','gy'}, use_global_device_ids=true, to_apply=%region_1.2.clone | all-reduce | flops 3072 | bytes 24576
  (380 shorter events, 324.0 us)
Async XLA Ops:
  163.6 11.1 %collective-permute-start.18 = (f32[3,1,1,128]{3,2,0,1:T(1,128)S(1)}, f32[3,1,1,128]{3,2,0,1:T(1,128)S(1)}, u32[]{:S(2)}, u32[]{:S(2)}) collective-permute-start(f32[3,1,1,128]{3,2,0,1:T(1,128)S(1)} %get-tuple-element.810), channel_id=1, source_target_pairs={{0,1},{1,2},{2,3},{3,4},{4,5},{5,6},{6,7},{7,8},{8,9},{9,10},{10,1... | collective-permute-start | bytes 4616 | tf_op jit(solution)/shard_map/while/body/eval_jaxpr/ppermute | solution.py:14
  166.8 7.9 %collective-permute-start.19 = (f32[3,1,1,128]{3,2,0,1:T(1,128)S(1)}, f32[3,1,1,128]{3,2,0,1:T(1,128)S(1)}, u32[]{:S(2)}, u32[]{:S(2)}) collective-permute-start(f32[3,1,1,128]{3,2,0,1:T(1,128)S(1)} %get-tuple-element.811), channel_id=1, source_target_pairs={{1,0},{2,1},{3,2},{4,3},{5,4},{6,5},{7,6},{8,7},{9,8},{10,9},{11,1... | collective-permute-start | bytes 4616 | tf_op jit(solution)/shard_map/while/body/eval_jaxpr/ppermute | solution.py:15
  172.8 9.2 %collective-permute-start.47 = (f32[3,1,1,128]{3,2,0,1:T(1,128)S(1)}, f32[3,1,1,128]{3,2,0,1:T(1,128)S(1)}, u32[]{:S(2)}, u32[]{:S(2)}) collective-permute-start(f32[3,1,1,128]{3,2,0,1:T(1,128)S(1)} %get-tuple-element.1158), channel_id=1, source_target_pairs={{1,0},{2,1},{3,2},{4,3},{5,4},{6,5},{7,6},{8,7},{9,8},{10,9},{11,1... | collective-permute-start | bytes 4616 | tf_op jit(solution)/shard_map/while/body/eval_jaxpr/ppermute | solution.py:15
  182.1 10.1 %collective-permute-start.20 = (f32[3,1,64,128]{3,2,0,1:T(8,128)S(1)}, f32[3,1,64,128]{3,2,0,1:T(8,128)S(1)}, u32[]{:S(2)}, u32[]{:S(2)}) collective-permute-start(f32[3,1,64,128]{3,2,0,1:T(8,128)S(1)} %get-tuple-element.649), channel_id=1, source_target_pairs={{0,32},{32,64},{64,96},{96,128},{128,160},{160,192},{192,224},{1,3... | collective-permute-start | bytes 294920 | tf_op jit(solution)/shard_map/ppermute | solution.py:23
  294.1 16.1 %collective-permute-start.67 = (f32[3,1,1,128]{3,2,0,1:T(1,128)S(1)}, f32[3,1,1,128]{3,2,0,1:T(1,128)S(1)}, u32[]{:S(2)}, u32[]{:S(2)}) collective-permute-start(f32[3,1,1,128]{3,2,0,1:T(1,128)S(1)} %get-tuple-element.1047), channel_id=1, source_target_pairs={{0,1},{1,2},{2,3},{3,4},{4,5},{5,6},{6,7},{7,8},{8,9},{9,10},{10,1... | collective-permute-start | bytes 4616 | tf_op jit(solution)/shard_map/while/body/eval_jaxpr/ppermute | solution.py:14
  297.7 14.5 %collective-permute-start.68 = (f32[3,1,1,128]{3,2,0,1:T(1,128)S(1)}, f32[3,1,1,128]{3,2,0,1:T(1,128)S(1)}, u32[]{:S(2)}, u32[]{:S(2)}) collective-permute-start(f32[3,1,1,128]{3,2,0,1:T(1,128)S(1)} %get-tuple-element.1048), channel_id=1, source_target_pairs={{1,0},{2,1},{3,2},{4,3},{5,4},{6,5},{7,6},{8,7},{9,8},{10,9},{11,1... | collective-permute-start | bytes 4616 | tf_op jit(solution)/shard_map/while/body/eval_jaxpr/ppermute | solution.py:15
  299.6 12.7 %collective-permute-start.21 = (f32[3,1,1,128]{3,2,0,1:T(1,128)S(1)}, f32[3,1,1,128]{3,2,0,1:T(1,128)S(1)}, u32[]{:S(2)}, u32[]{:S(2)}) collective-permute-start(f32[3,1,1,128]{3,2,0,1:T(1,128)S(1)} %get-tuple-element.793), channel_id=1, source_target_pairs={{0,1},{1,2},{2,3},{3,4},{4,5},{5,6},{6,7},{7,8},{8,9},{9,10},{10,1... | collective-permute-start | bytes 4616 | tf_op jit(solution)/shard_map/while/body/eval_jaxpr/ppermute | solution.py:14
  317.9 7.9 %collective-permute-start.69 = (f32[3,1,64,128]{3,2,0,1:T(8,128)S(1)}, f32[3,1,64,128]{3,2,0,1:T(8,128)S(1)}, u32[]{:S(2)}, u32[]{:S(2)}) collective-permute-start(f32[3,1,64,128]{3,2,0,1:T(8,128)S(1)} %get-tuple-element.579), channel_id=1, source_target_pairs={{32,0},{64,32},{96,64},{128,96},{160,128},{192,160},{224,192},{33,... | collective-permute-start | bytes 294920 | tf_op jit(solution)/shard_map/ppermute | solution.py:23
  348.4 9.3 %collective-permute-start.29 = (f32[3,1,1,128]{3,2,0,1:T(1,128)S(1)}, f32[3,1,1,128]{3,2,0,1:T(1,128)S(1)}, u32[]{:S(2)}, u32[]{:S(2)}) collective-permute-start(f32[3,1,1,128]{3,2,0,1:T(1,128)S(1)} %get-tuple-element.759), channel_id=1, source_target_pairs={{0,1},{1,2},{2,3},{3,4},{4,5},{5,6},{6,7},{7,8},{8,9},{9,10},{10,1... | collective-permute-start | bytes 4616 | tf_op jit(solution)/shard_map/while/body/eval_jaxpr/ppermute | solution.py:14
  363.8 8.6 %collective-permute-start.73 = (f32[3,1,1,128]{3,2,0,1:T(1,128)S(1)}, f32[3,1,1,128]{3,2,0,1:T(1,128)S(1)}, u32[]{:S(2)}, u32[]{:S(2)}) collective-permute-start(f32[3,1,1,128]{3,2,0,1:T(1,128)S(1)} %get-tuple-element.996), channel_id=1, source_target_pairs={{0,1},{1,2},{2,3},{3,4},{4,5},{5,6},{6,7},{7,8},{8,9},{9,10},{10,1... | collective-permute-start | bytes 4616 | tf_op jit(solution)/shard_map/while/body/eval_jaxpr/ppermute | solution.py:14
  369.2 8.3 %collective-permute-start.74 = (f32[3,1,1,128]{3,2,0,1:T(1,128)S(1)}, f32[3,1,1,128]{3,2,0,1:T(1,128)S(1)}, u32[]{:S(2)}, u32[]{:S(2)}) collective-permute-start(f32[3,1,1,128]{3,2,0,1:T(1,128)S(1)} %get-tuple-element.997), channel_id=1, source_target_pairs={{1,0},{2,1},{3,2},{4,3},{5,4},{6,5},{7,6},{8,7},{9,8},{10,9},{11,1... | collective-permute-start | bytes 4616 | tf_op jit(solution)/shard_map/while/body/eval_jaxpr/ppermute | solution.py:15
  378.5 11.1 %collective-permute-start.32 = (f32[3,1,1,128]{3,2,0,1:T(1,128)S(1)}, f32[3,1,1,128]{3,2,0,1:T(1,128)S(1)}, u32[]{:S(2)}, u32[]{:S(2)}) collective-permute-start(f32[3,1,1,128]{3,2,0,1:T(1,128)S(1)} %get-tuple-element.742), channel_id=1, source_target_pairs={{0,1},{1,2},{2,3},{3,4},{4,5},{5,6},{6,7},{7,8},{8,9},{9,10},{10,1... | collective-permute-start | bytes 4616 | tf_op jit(solution)/shard_map/while/body/eval_jaxpr/ppermute | solution.py:14
  395.1 7.8 %collective-permute-start.76 = (f32[3,1,1,128]{3,2,0,1:T(1,128)S(1)}, f32[3,1,1,128]{3,2,0,1:T(1,128)S(1)}, u32[]{:S(2)}, u32[]{:S(2)}) collective-permute-start(f32[3,1,1,128]{3,2,0,1:T(1,128)S(1)} %get-tuple-element.979), channel_id=1, source_target_pairs={{0,1},{1,2},{2,3},{3,4},{4,5},{5,6},{6,7},{7,8},{8,9},{9,10},{10,1... | collective-permute-start | bytes 4616 | tf_op jit(solution)/shard_map/while/body/eval_jaxpr/ppermute | solution.py:14
  408.4 7.9 %collective-permute-start.35 = (f32[3,1,1,128]{3,2,0,1:T(1,128)S(1)}, f32[3,1,1,128]{3,2,0,1:T(1,128)S(1)}, u32[]{:S(2)}, u32[]{:S(2)}) collective-permute-start(f32[3,1,1,128]{3,2,0,1:T(1,128)S(1)} %get-tuple-element.725), channel_id=1, source_target_pairs={{0,1},{1,2},{2,3},{3,4},{4,5},{5,6},{6,7},{7,8},{8,9},{9,10},{10,1... | collective-permute-start | bytes 4616 | tf_op jit(solution)/shard_map/while/body/eval_jaxpr/ppermute | solution.py:14
  422.0 8.3 %collective-permute-start.79 = (f32[3,1,1,128]{3,2,0,1:T(1,128)S(1)}, f32[3,1,1,128]{3,2,0,1:T(1,128)S(1)}, u32[]{:S(2)}, u32[]{:S(2)}) collective-permute-start(f32[3,1,1,128]{3,2,0,1:T(1,128)S(1)} %get-tuple-element.962), channel_id=1, source_target_pairs={{0,1},{1,2},{2,3},{3,4},{4,5},{5,6},{6,7},{7,8},{8,9},{9,10},{10,1... | collective-permute-start | bytes 4616 | tf_op jit(solution)/shard_map/while/body/eval_jaxpr/ppermute | solution.py:14
  435.9 7.8 %collective-permute-start.38 = (f32[3,1,1,128]{3,2,0,1:T(1,128)S(1)}, f32[3,1,1,128]{3,2,0,1:T(1,128)S(1)}, u32[]{:S(2)}, u32[]{:S(2)}) collective-permute-start(f32[3,1,1,128]{3,2,0,1:T(1,128)S(1)} %get-tuple-element.708), channel_id=1, source_target_pairs={{0,1},{1,2},{2,3},{3,4},{4,5},{5,6},{6,7},{7,8},{8,9},{9,10},{10,1... | collective-permute-start | bytes 4616 | tf_op jit(solution)/shard_map/while/body/eval_jaxpr/ppermute | solution.py:14
  449.3 8.2 %collective-permute-start.82 = (f32[3,1,1,128]{3,2,0,1:T(1,128)S(1)}, f32[3,1,1,128]{3,2,0,1:T(1,128)S(1)}, u32[]{:S(2)}, u32[]{:S(2)}) collective-permute-start(f32[3,1,1,128]{3,2,0,1:T(1,128)S(1)} %get-tuple-element.954), channel_id=1, source_target_pairs={{0,1},{1,2},{2,3},{3,4},{4,5},{5,6},{6,7},{7,8},{8,9},{9,10},{10,1... | collective-permute-start | bytes 4616 | tf_op jit(solution)/shard_map/while/body/eval_jaxpr/ppermute | solution.py:14
  463.0 9.9 %collective-permute-start.41 = (f32[3,1,1,128]{3,2,0,1:T(1,128)S(1)}, f32[3,1,1,128]{3,2,0,1:T(1,128)S(1)}, u32[]{:S(2)}, u32[]{:S(2)}) collective-permute-start(f32[3,1,1,128]{3,2,0,1:T(1,128)S(1)} %get-tuple-element.691), channel_id=1, source_target_pairs={{0,1},{1,2},{2,3},{3,4},{4,5},{5,6},{6,7},{7,8},{8,9},{9,10},{10,1... | collective-permute-start | bytes 4616 | tf_op jit(solution)/shard_map/while/body/eval_jaxpr/ppermute | solution.py:14
  478.6 9.9 %collective-permute-start.85 = (f32[3,1,1,128]{3,2,0,1:T(1,128)S(1)}, f32[3,1,1,128]{3,2,0,1:T(1,128)S(1)}, u32[]{:S(2)}, u32[]{:S(2)}) collective-permute-start(f32[3,1,1,128]{3,2,0,1:T(1,128)S(1)} %get-tuple-element.937), channel_id=1, source_target_pairs={{0,1},{1,2},{2,3},{3,4},{4,5},{5,6},{6,7},{7,8},{8,9},{9,10},{10,1... | collective-permute-start | bytes 4616 | tf_op jit(solution)/shard_map/while/body/eval_jaxpr/ppermute | solution.py:14
  494.1 9.9 %collective-permute-start.87 = (f32[3,1,64,128]{3,2,0,1:T(8,128)S(1)}, f32[3,1,64,128]{3,2,0,1:T(8,128)S(1)}, u32[]{:S(2)}, u32[]{:S(2)}) collective-permute-start(f32[3,1,64,128]{3,2,0,1:T(8,128)S(1)} %get-tuple-element.596), channel_id=1, source_target_pairs={{32,0},{64,32},{96,64},{128,96},{160,128},{192,160},{224,192},{33,... | collective-permute-start | bytes 294920 | tf_op jit(solution)/shard_map/ppermute | solution.py:23
  495.4 16.6 %collective-permute-start.44 = (f32[3,1,1,128]{3,2,0,1:T(1,128)S(1)}, f32[3,1,1,128]{3,2,0,1:T(1,128)S(1)}, u32[]{:S(2)}, u32[]{:S(2)}) collective-permute-start(f32[3,1,1,128]{3,2,0,1:T(1,128)S(1)} %get-tuple-element.674), channel_id=1, source_target_pairs={{0,1},{1,2},{2,3},{3,4},{4,5},{5,6},{6,7},{7,8},{8,9},{9,10},{10,1... | collective-permute-start | bytes 4616 | tf_op jit(solution)/shard_map/while/body/eval_jaxpr/ppermute | solution.py:14
  502.1 10.0 %collective-permute-start.45 = (f32[3,1,1,128]{3,2,0,1:T(1,128)S(1)}, f32[3,1,1,128]{3,2,0,1:T(1,128)S(1)}, u32[]{:S(2)}, u32[]{:S(2)}) collective-permute-start(f32[3,1,1,128]{3,2,0,1:T(1,128)S(1)} %get-tuple-element.684), channel_id=1, source_target_pairs={{1,0},{2,1},{3,2},{4,3},{5,4},{6,5},{7,6},{8,7},{9,8},{10,9},{11,1... | collective-permute-start | bytes 4616 | tf_op jit(solution)/shard_map/while/body/eval_jaxpr/ppermute | solution.py:15
  504.1 8.0 %collective-permute-start.88 = (f32[3,1,1,128]{3,2,0,1:T(1,128)S(1)}, f32[3,1,1,128]{3,2,0,1:T(1,128)S(1)}, u32[]{:S(2)}, u32[]{:S(2)}) collective-permute-start(f32[3,1,1,128]{3,2,0,1:T(1,128)S(1)} %get-tuple-element.920), channel_id=1, source_target_pairs={{0,1},{1,2},{2,3},{3,4},{4,5},{5,6},{6,7},{7,8},{8,9},{9,10},{10,1... | collective-permute-start | bytes 4616 | tf_op jit(solution)/shard_map/while/body/eval_jaxpr/ppermute | solution.py:14
  510.1 7.9 %collective-permute-start.89 = (f32[3,1,1,128]{3,2,0,1:T(1,128)S(1)}, f32[3,1,1,128]{3,2,0,1:T(1,128)S(1)}, u32[]{:S(2)}, u32[]{:S(2)}) collective-permute-start(f32[3,1,1,128]{3,2,0,1:T(1,128)S(1)} %get-tuple-element.921), channel_id=1, source_target_pairs={{1,0},{2,1},{3,2},{4,3},{5,4},{6,5},{7,6},{8,7},{9,8},{10,9},{11,1... | collective-permute-start | bytes 4616 | tf_op jit(solution)/shard_map/while/body/eval_jaxpr/ppermute | solution.py:15
  (74 other events, 664.4 us)
where the time goes:
time: 629 us; the launch traced here: 627 us
  starting transfers between devices  281 us (45%)
  blocking collectives  175 us (28%)
  waiting for transfers between devices  149 us (24%)
  local copies, waits for them, and re-layouts  10.7 us (2%)
  other arithmetic  7.24 us (1%)
    ppermute x31, starting transfers between devices, with_halo(): before = lax.ppermute(last, axis, up)  144 us
    unnamed x1, blocking collectives  102 us
    ppermute x31, waiting for transfers between devices, with_halo(): after = lax.ppermute(first, axis, down)  93.3 us
    ppermute x28, starting transfers between devices, passed_along(): return lax.ppermute(block, axis, route)  77 us
    all_gather x1, blocking collectives, per_device(): all_wells = lax.all_gather(well_adjoint, ('gx', 'gy'), axis=1, tiled=True)  73 us
    ppermute x31, starting transfers between devices, with_halo(): after = lax.ppermute(first, axis, down)  59.5 us
    ppermute x28, waiting for transfers between devices, passed_along(): return lax.ppermute(block, axis, route)  54.6 us
  transfers between devices with their start and end apart: 90, of which 53 were waited for; matrix products, arithmetic and copies ran while one was open for 0% of the time, Pallas kernels for 0%

commit v1 on v0

v1 whole, which is shorter than its diff:
```python
import functools

import jax
import jax.numpy as jnp
from jax import lax
from jax.experimental import pallas as pl
from jax.experimental.pallas import tpu as pltpu
from jax.sharding import PartitionSpec as P

F32 = jnp.float32
BF16 = jnp.bfloat16
PLANES = 8
LINES = 64
ZC = 16
PAIRS = 14
STRIP = 16
VMEM_LIMIT = 24 * 1024 * 1024

VMEM = pl.BlockSpec(memory_space=pltpu.VMEM)
SMEM = pl.BlockSpec(memory_space=pltpu.SMEM)


def split3(x):
    hi = x.astype(BF16).astype(F32)
    rest = x - hi
    mid = rest.astype(BF16).astype(F32)
    lo = rest - mid
    return hi, mid, lo


def split_rows(x):
    return jnp.concatenate(split3(x), axis=0).astype(BF16)


def join_rows(y, rows):
    return y[0:rows] + y[rows : 2 * rows] + y[2 * rows : 3 * rows]


def lane_iota(rows):
    return lax.broadcasted_iota(jnp.int32, (rows, 128), 1)


def row_iota(rows):
    return lax.broadcasted_iota(jnp.int32, (rows, 128), 0)


def roll_lanes(x, shift):
    shift %= 128
    return x if shift == 0 else pltpu.roll(x, shift, 1)


def pack_kernel(me_ref, rhs, einv, xc, yc, *rest):
    outs, turned = rest[:PLANES], rest[PLANES]
    me = me_ref[0]
    arrays = (
        [(rhs, i) for i in range(6)]
        + [(einv, i) for i in range(9)]
        + [(xc, i) for i in range(6)]
        + [(yc, i) for i in range(6)]
    )
    for g in range(PAIRS):
        ref, i = arrays[2 * g]
        top = ref[i]
        if 2 * g + 1 < len(arrays):
            ref, i = arrays[2 * g + 1]
            low = ref[i]
        else:
            low = jnp.zeros((LINES, 128), F32)
        turned[g] = jnp.concatenate([top, low], axis=0).T
    for d in range(PLANES):
        target = (me + d) & 7
        outs[d][...] = turned[:, pl.ds(pl.multiple_of(target * ZC, ZC), ZC), :]


def perf_tiles(zrefs):
    half = lane_iota(8) < 64
    return [
        jnp.where(half, zrefs[2 * j][...], roll_lanes(zrefs[2 * j + 1][...], 64))
        for j in range(PLANES // 2)
    ]


def source_kernel(me_ref, *rest):
    zrefs, (src_ref, pick_ref) = rest[:PLANES], rest[PLANES:]
    me = me_ref[0]
    tiles = perf_tiles(zrefs)
    lane = lane_iota(128)
    row = row_iota(128)
    wells = [t[4:5].astype(jnp.int32) for t in tiles]
    picked = [jnp.zeros((32, 128), F32) for _ in tiles]
    for d in range(PLANES):
        base = ((me - d) & 7) * 128
        values = zrefs[d][...]
        parts = jnp.concatenate(list(split3(values)) + [jnp.zeros((8, 128), F32)], axis=0).astype(BF16)
        for j in range(4):
            hot = jnp.where(wells[j] == row + base, 1.0, 0.0).astype(BF16)
            pick_ref[d, :, 128 * j : 128 * j + 128] = hot
            picked[j] += jnp.dot(parts, hot, preferred_element_type=F32)
    half = lane_iota(1) < 64
    depth_row = row_iota(ZC)
    low = lane_iota(ZC) < 64
    for j in range(4):
        term = join_rows(picked[j], 8)[0:3] * tiles[j][5:6]
        cell = tiles[j][3:4].astype(jnp.int32)
        at_z = (cell & 127) == depth_row + me * ZC
        at_y = jnp.where(((cell >> 7) & 63) == row, 1.0, 0.0).astype(BF16)
        rows = []
        for side in range(2):
            keep = jnp.logical_and(at_z, half if side == 0 else jnp.logical_not(half))
            rows += [jnp.where(keep, term[c : c + 1], 0.0) for c in range(3)]
        left = split_rows(jnp.concatenate(rows, axis=0))
        spread = lax.dot_general(left, at_y, (((1,), (1,)), ((), ())), preferred_element_type=F32)
        spread = join_rows(spread, 96)
        for side in range(2):
            c0, c1, c2 = (spread[48 * side + 16 * c : 48 * side + 16 * c + 16] for c in range(3))
            d = 2 * j + side
            src_ref[d, 0] = jnp.where(low, c0, roll_lanes(c1, 64))
            src_ref[d, 1] = jnp.where(low, c2, roll_lanes(c0, 64))
            src_ref[d, 2] = jnp.where(low, c1, roll_lanes(c2, 64))


def strip_kernel(*rest):
    chunks, src, (first_ref, last_ref) = rest[:PLANES], rest[PLANES], rest[PLANES + 1 :]
    slot = (lane_iota(ZC) & 63) >> 4
    for q in range(PLANES * PAIRS // 4):
        first = last = None
        for s in range(4):
            d, g = divmod(4 * q + s, PAIRS)
            x = chunks[d][g]
            if g < 3:
                x = x + src[d, g]
            a = roll_lanes(x, 16 * s)
            b = roll_lanes(x, 16 * s + 80)
            first = a if s == 0 else jnp.where(slot == s, a, first)
            last = b if s == 0 else jnp.where(slot == s, b, last)
        first_ref[q] = first
        last_ref[q] = last


def block_apply(blocks, v):
    return [blocks[3 * a] * v[0] + blocks[3 * a + 1] * v[1] + blocks[3 * a + 2] * v[2] for a in range(3)]


def plane_apply(blocks, lower, upper, v):
    w = block_apply(blocks, v)
    u = [v[c] - lower[c] * roll_lanes(w[c], 1) - upper[c] * roll_lanes(w[c], 127) for c in range(3)]
    return block_apply(blocks, u)


def march_kernel(me_ref, *rest):
    chunks, rest = rest[:PLANES], rest[PLANES:]
    zrefs, rest = rest[:PLANES], rest[PLANES:]
    (src, before, after, pick_ref), rest = rest[:4], rest[4:]
    outs, (grid, field) = rest[:PLANES], rest[PLANES:]
    me = me_ref[0]
    lane = lane_iota(ZC)
    own = lane < 64
    right = lane < 80
    left = lane >= 112

    for d in range(PLANES):
        plane = (me - d) & 7
        for g in range(PAIRS):
            q, s = divmod(PAIRS * d + g, 4)
            x = chunks[d][g]
            if g < 3:
                x = x + src[d, g]
            for h in range(2):
                n = 2 * g + h
                if n == 27:
                    continue
                at = 16 * s + 64 * h
                edge = jnp.where(right, roll_lanes(after[q], 64 - at), roll_lanes(before[q], 112 - at))
                edge = jnp.where(jnp.logical_or(right, left), edge, 0.0)
                grid[plane, n] = jnp.where(own, roll_lanes(x, 64 * h), edge)

    for t in range(2):
        rows = slice(8 * t, 8 * t + 8)
        state = None
        for i in range(PLANES):
            blocks = [grid[i, 6 + n, rows] for n in range(9)]
            lower = [grid[i, 21 + c, rows] for c in range(3)]
            upper = [grid[i, 24 + c, rows] for c in range(3)]
            new = []
            for k in range(2):
                v = [grid[i, 3 * k + c, rows] for c in range(3)]
                if i > 0:
                    v = [v[c] - grid[i, 15 + c, rows] * state[k][c] for c in range(3)]
                new.append(plane_apply(blocks, lower, upper, v))
            state = new
            for k in range(2):
                for c in range(3):
                    field[i, 3 * k + c, rows] = state[k][c]
        for i in range(PLANES - 2, -1, -1):
            blocks = [grid[i, 6 + n, rows] for n in range(9)]
            lower = [grid[i, 21 + c, rows] for c in range(3)]
            upper = [grid[i, 24 + c, rows] for c in range(3)]
            new = []
            for k in range(2):
                v = [grid[i, 18 + c, rows] * state[k][c] for c in range(3)]
                p = plane_apply(blocks, lower, upper, v)
                new.append([field[i, 3 * k + c, rows] - p[c] for c in range(3)])
            state = new
            for k in range(2):
                for c in range(3):
                    field[i, 3 * k + c, rows] = state[k][c]

    for d in range(PLANES):
        plane = (me + d) & 7
        for c in range(3):
            pair = jnp.where(own, field[plane, c], roll_lanes(field[plane, 3 + c], 64))
            outs[d][2 * c] = pair[0:8]
            outs[d][2 * c + 1] = pair[8:16]

    tiles = perf_tiles(zrefs)
    row = row_iota(128)
    depth_row = row_iota(ZC)
    half = lane_iota(1) < 64
    parts = []
    for j in range(4):
        cell = tiles[j][3:4].astype(jnp.int32)
        at_z = (cell & 127) == depth_row + me * ZC
        at_y = jnp.where(((cell >> 7) & 63) == row, 1.0, 0.0).astype(BF16)
        total = None
        for side in range(2):
            plane = (me - 2 * j - side) & 7
            x = jnp.concatenate([field[plane, 3 + c] for c in range(3)], axis=0)
            got = join_rows(jnp.dot(split_rows(x), at_y, preferred_element_type=F32), 48)
            keep = jnp.logical_and(at_z, half if side == 0 else jnp.logical_not(half))
            got = [jnp.where(keep, got[16 * c : 16 * c + 16], 0.0) for c in range(3)]
            total = got if total is None else [a + b for a, b in zip(total, got)]
        value = [jnp.sum(t, axis=0, keepdims=True) * tiles[j][5:6] for t in total]
        value = jnp.concatenate(value + [jnp.zeros((5, 128), F32)], axis=0)
        parts.append(
            jnp.concatenate(list(split3(value)) + [jnp.zeros((8, 128), F32)], axis=0).astype(BF16)
        )
    parts = jnp.concatenate(parts, axis=1)
    for d in range(PLANES):
        sums = lax.dot_general(
            parts, pick_ref[(PLANES - d) % PLANES], (((1,), (1,)), ((), ())), preferred_element_type=F32
        )
        outs[d][6] = join_rows(sums, 8)


def unpack_kernel(me_ref, *rest):
    chunks, (out, turned) = rest[:PLANES], rest[PLANES:]
    me = me_ref[0]
    for d in range(PLANES):
        start = ((me - d) & 7) * ZC
        for c in range(3):
            for t in range(2):
                turned[c, pl.ds(pl.multiple_of(start + 8 * t, 8), 8), :] = chunks[d][2 * c + t]
    for c in range(3):
        y = turned[c].T
        out[0, c] = y[0:LINES]
        out[1, c] = y[LINES : 2 * LINES]


def call(kernel, inputs, out_shape, scratch=()):
    return pl.pallas_call(
        kernel,
        out_shape=out_shape,
        in_specs=[SMEM if x.ndim == 1 else VMEM for x in inputs],
        out_specs=jax.tree.map(lambda _: VMEM, out_shape),
        scratch_shapes=list(scratch),
        compiler_params=pltpu.CompilerParams(vmem_limit_bytes=VMEM_LIMIT),
    )(*inputs)


def shift_gx(x, d):
    n = lax.axis_size("gx")
    return lax.ppermute(x, "gx", [(i, (i + d) % n) for i in range(n)])


def radices(size):
    out = []
    while size > 1:
        r = 4 if size % 4 == 0 and size != 8 else 2
        out.append(r)
        size //= r
    return out


def sum_gy(x):
    size = lax.axis_size("gy")
    stride = 1
    for radix in reversed(radices(size)):
        total = x
        for k in range(1, radix):
            route = []
            for b in range(size):
                digit = (b // stride) % radix
                route.append((b, b + ((digit + k) % radix - digit) * stride))
            total = total + lax.ppermute(x, "gy", route)
        x = total
        stride *= radix
    return x


EXCHANGE_ORDER = (4, 3, 5, 2, 6, 1, 7)


def per_device(
    adjoint_rhs, block_inverse, x_couplings, y_couplings, perf_cell, perf_well, perf_weight, well_adjoint
):
    me = lax.axis_index("gx").astype(jnp.int32)
    line_block = lax.axis_index("gy")
    me_arr = me.reshape(1)
    held = well_adjoint.shape[1]

    chunk = jax.ShapeDtypeStruct((PAIRS, ZC, 128), F32)
    packed = call(
        pack_kernel,
        [
            me_arr,
            adjoint_rhs.reshape(6, LINES, 128),
            block_inverse.reshape(9, LINES, 128),
            x_couplings.reshape(6, LINES, 128),
            y_couplings.reshape(6, LINES, 128),
        ],
        [chunk] * PLANES,
        [pltpu.VMEM((PAIRS, 128, 128), F32)],
    )
    chunks = [packed[0]] + [None] * 7
    for d in EXCHANGE_ORDER:
        chunks[d] = shift_gx(packed[d], d)

    wells = lax.dynamic_update_slice(jnp.zeros((8, 128), F32), well_adjoint, (0, held * line_block))
    wells = sum_gy(wells)
    perfs = jnp.stack([perf_cell.astype(F32), perf_well.astype(F32), perf_weight])
    wells = wells + jnp.pad(perfs, ((3, 2), (0, 64)))
    tiles = [wells] + [shift_gx(wells, d) for d in range(1, PLANES)]

    src, pick = call(
        source_kernel,
        [me_arr] + tiles,
        [
            jax.ShapeDtypeStruct((PLANES, 3, ZC, 128), F32),
            jax.ShapeDtypeStruct((PLANES, 128, 512), BF16),
        ],
    )

    strip = jax.ShapeDtypeStruct((PLANES * PAIRS // 4, ZC, 128), F32)
    first, last = call(strip_kernel, chunks + [src], [strip, strip])
    lines = lax.axis_size("gy")
    up = [(i, i + 1) for i in range(lines - 1)]
    before = lax.ppermute(last, "gy", up)
    after = lax.ppermute(first, "gy", [(j, i) for i, j in up])

    back = call(
        march_kernel,
        [me_arr] + chunks + tiles + [src, before, after, pick],
        [jax.ShapeDtypeStruct((7, 8, 128), F32)] * PLANES,
        [pltpu.VMEM((PLANES, 27, ZC, 128), F32), pltpu.VMEM((PLANES, 6, ZC, 128), F32)],
    )
    got = [back[0]] + [None] * 7
    for d in EXCHANGE_ORDER:
        got[d] = shift_gx(back[d], d)

    precond = call(
        unpack_kernel,
        [me_arr] + got,
        jax.ShapeDtypeStruct((2, 3, LINES, 128), F32),
        [pltpu.VMEM((3, 128, 128), F32)],
    ).reshape(adjoint_rhs.shape)
    sums = got[0][6]
    for d in range(1, PLANES):
        sums = sums + got[d][6]
    sums = sum_gy(sums)
    well_update = lax.dynamic_slice(sums, (0, held * line_block), (3, held))
    return precond, well_update


def solution(mesh):
    placed = (
        P(None, None, "gx", "gy", None),
        P(None, None, "gx", "gy", None),
        P(None, None, "gx", "gy", None),
        P(None, None, "gx", "gy", None),
        P(("gx", "gy")),
        P(("gx", "gy")),
        P(("gx", "gy")),
        P(None, ("gx", "gy")),
    )
    return jax.shard_map(
        per_device,
        mesh=mesh,
        in_specs=placed,
        out_specs=(P(None, None, "gx", "gy", None), P(None, ("gx", "gy"))),
        check_vma=False,
    )
```

time: 629 us -> 116 us (0.18)
  the two profiles are of different devices: /device:TPU:1 before, /device:TPU:6 now
where the time goes in v1:
time: 116 us
  starting transfers between devices  68 us (59%)
  waiting for transfers between devices  34.4 us (30%)
  local copies, waits for them, and re-layouts  6.52 us (6%)
  Pallas kernels  6.02 us (5%)
    ppermute x21, starting transfers between devices, shift_gx(): return lax.ppermute(x, 'gx', [(i, (i + d) % n) for i in range(n)])  46.5 us
    ppermute x14, waiting for transfers between devices, sum_gy(): total = total + lax.ppermute(x, 'gy', route)  18.2 us
    ppermute x14, starting transfers between devices, sum_gy(): total = total + lax.ppermute(x, 'gy', route)  15.9 us
    ppermute x21, waiting for transfers between devices, shift_gx(): return lax.ppermute(x, 'gx', [(i, (i + d) % n) for i in range(n)])  12.6 us
    pallas_call x5, Pallas kernels, call(): pl.pallas_call(kernel, out_shape=out_shape, in_specs=[SMEM if x.ndim == 1...  6.02 us
    unnamed x16, local copies, waits for them, and re-layouts  5.07 us
    ppermute x1, starting transfers between devices, per_device(): after = lax.ppermute(first, 'gy', [(j, i) for i, j in up])  3.64 us
  transfers between devices with their start and end apart: 37, of which 18 were waited for; matrix products, arithmetic and copies ran while one was open for 0% of the time, Pallas kernels for 2%

profile of v1, /device:TPU:6, one launch (start us, length us, event | category | flops | bytes accessed | tf_op | source)
XLA Modules:
  0.0 115.8 jit_solution(14050295439564553158)
XLA Ops:
  12.8 1.9 %collective-permute-start = (f32[14,16,128]{2,1,0:T(8,128)S(1)}, f32[14,16,128]{2,1,0:T(8,128)S(1)}, u32[]{:S(2)}, u32[]{:S(2)}) collective-permute-start(f32[14,16,128]{2,1,0:T(8,128)S(1)} %get-tuple-element.23), channel_id=1, source_target_pairs={{0,32},{32,64},{64,96},{96,128},{128,160},{160,192},{192,224},{224... | collective-permute-start | bytes 344072 | tf_op jit(solution)/shard_map/ppermute | solution.py:272
  14.7 3.3 %collective-permute-start.1 = (f32[14,16,128]{2,1,0:T(8,128)S(1)}, f32[14,16,128]{2,1,0:T(8,128)S(1)}, u32[]{:S(2)}, u32[]{:S(2)}) collective-permute-start(f32[14,16,128]{2,1,0:T(8,128)S(1)} %get-tuple-element.24), channel_id=1, source_target_pairs={{0,64},{32,96},{64,128},{96,160},{128,192},{160,224},{192,0},{224,... | collective-permute-start | bytes 344072 | tf_op jit(solution)/shard_map/ppermute | solution.py:272
  17.9 3.0 %collective-permute-start.13 = (f32[8,128]{1,0:T(8,128)S(1)}, f32[8,128]{1,0:T(8,128)S(1)}, u32[]{:S(2)}, u32[]{:S(2)}) collective-permute-start(f32[8,128]{1,0:T(8,128)S(1)} %add.83), channel_id=1, source_target_pairs={{0,24},{1,25},{2,26},{3,27},{4,28},{5,29},{6,30},{7,31},{8,0},{9,1... | collective-permute-start | bytes 12296 | tf_op jit(solution)/shard_map/ppermute | solution.py:294
  22.6 3.5 %collective-permute-done.12 = f32[8,128]{1,0:T(8,128)S(1)} collective-permute-done((f32[8,128]{1,0:T(8,128)S(1)}, f32[8,128]{1,0:T(8,128)S(1)}, u32[]{:S(2)}, u32[]{:S(2)}) %collective-permute-start.12) | collective-permute-done | bytes 4128 | tf_op jit(solution)/shard_map/ppermute | solution.py:294
  28.5 2.4 %collective-permute-start.19 = (f32[8,128]{1,0:T(8,128)S(1)}, f32[8,128]{1,0:T(8,128)S(1)}, u32[]{:S(2)}, u32[]{:S(2)}) collective-permute-start(f32[8,128]{1,0:T(8,128)S(1)} %fusion.1.rest_0_.rest_8_), channel_id=1, source_target_pairs={{0,192},{32,224},{64,0},{96,32},{128,64},{160,96},{192,128},{224,1... | collective-permute-start | bytes 12296 | tf_op jit(solution)/shard_map/ppermute | solution.py:272
  30.8 4.0 %collective-permute-start.18 = (f32[8,128]{1,0:T(8,128)S(1)}, f32[8,128]{1,0:T(8,128)S(1)}, u32[]{:S(2)}, u32[]{:S(2)}) collective-permute-start(f32[8,128]{1,0:T(8,128)S(1)} %fusion.1.rest_0_.rest_8_), channel_id=1, source_target_pairs={{0,160},{32,192},{64,224},{96,0},{128,32},{160,64},{192,96},{224,1... | collective-permute-start | bytes 12296 | tf_op jit(solution)/shard_map/ppermute | solution.py:272
  35.9 3.3 %collective-permute-start.16 = (f32[8,128]{1,0:T(8,128)S(1)}, f32[8,128]{1,0:T(8,128)S(1)}, u32[]{:S(2)}, u32[]{:S(2)}) collective-permute-start(f32[8,128]{1,0:T(8,128)S(1)} %fusion.1.rest_0_.rest_8_), channel_id=1, source_target_pairs={{0,96},{32,128},{64,160},{96,192},{128,224},{160,0},{192,32},{224,... | collective-permute-start | bytes 12296 | tf_op jit(solution)/shard_map/ppermute | solution.py:272
  39.1 2.7 %collective-permute-start.15 = (f32[8,128]{1,0:T(8,128)S(1)}, f32[8,128]{1,0:T(8,128)S(1)}, u32[]{:S(2)}, u32[]{:S(2)}) collective-permute-start(f32[8,128]{1,0:T(8,128)S(1)} %fusion.1.rest_0_.rest_8_), channel_id=1, source_target_pairs={{0,64},{32,96},{64,128},{96,160},{128,192},{160,224},{192,0},{224,... | collective-permute-start | bytes 12296 | tf_op jit(solution)/shard_map/ppermute | solution.py:272
  44.9 4.2 %collective-permute-start.3 = (f32[14,16,128]{2,1,0:T(8,128)S(1)}, f32[14,16,128]{2,1,0:T(8,128)S(1)}, u32[]{:S(2)}, u32[]{:S(2)}) collective-permute-start(f32[14,16,128]{2,1,0:T(8,128)S(1)} %get-tuple-element.26), channel_id=1, source_target_pairs={{0,128},{32,160},{64,192},{96,224},{128,0},{160,32},{192,64},{224,... | collective-permute-start | bytes 344072 | tf_op jit(solution)/shard_map/ppermute | solution.py:272
  49.1 3.5 %collective-permute-start.4 = (f32[14,16,128]{2,1,0:T(8,128)S(1)}, f32[14,16,128]{2,1,0:T(8,128)S(1)}, u32[]{:S(2)}, u32[]{:S(2)}) collective-permute-start(f32[14,16,128]{2,1,0:T(8,128)S(1)} %get-tuple-element.27), channel_id=1, source_target_pairs={{0,160},{32,192},{64,224},{96,0},{128,32},{160,64},{192,96},{224,1... | collective-permute-start | bytes 344072 | tf_op jit(solution)/shard_map/ppermute | solution.py:272
  55.1 5.6 %collective-permute-done.4.rest_5_ = f32[14,16,128]{2,1,0:T(8,128)S(1)} collective-permute-done((f32[14,16,128]{2,1,0:T(8,128)S(1)}, f32[14,16,128]{2,1,0:T(8,128)S(1)}, u32[]{:S(2)}, u32[]{:S(2)}) %collective-permute-start.4) | collective-permute-done | bytes 114720 | tf_op jit(solution)/shard_map/ppermute | solution.py:272
  60.7 2.8 %collective-permute-done.5.rest_6_ = f32[14,16,128]{2,1,0:T(8,128)S(1)} collective-permute-done((f32[14,16,128]{2,1,0:T(8,128)S(1)}, f32[14,16,128]{2,1,0:T(8,128)S(1)}, u32[]{:S(2)}, u32[]{:S(2)}) %collective-permute-start.5) | collective-permute-done | bytes 114720 | tf_op jit(solution)/shard_map/ppermute | solution.py:272
  63.9 1.9 %collective-permute-start.21 = (f32[28,16,128]{2,1,0:T(8,128)S(1)}, f32[28,16,128]{2,1,0:T(8,128)S(1)}, u32[]{:S(2)}, u32[]{:S(2)}) collective-permute-start(f32[28,16,128]{2,1,0:T(8,128)S(1)} %get-tuple-element.31), channel_id=1, source_target_pairs={{0,1},{1,2},{2,3},{3,4},{4,5},{5,6},{6,7},{7,8},{8,9},{9,10},{10,1... | collective-permute-start | bytes 688136 | tf_op jit(solution)/shard_map/ppermute | solution.py:347
  65.9 3.6 %collective-permute-start.22 = (f32[28,16,128]{2,1,0:T(8,128)S(1)}, f32[28,16,128]{2,1,0:T(8,128)S(1)}, u32[]{:S(2)}, u32[]{:S(2)}) collective-permute-start(f32[28,16,128]{2,1,0:T(8,128)S(1)} %get-tuple-element.32), channel_id=1, source_target_pairs={{1,0},{2,1},{3,2},{4,3},{5,4},{6,5},{7,6},{8,7},{9,8},{10,9},{11,1... | collective-permute-start | bytes 688136 | tf_op jit(solution)/shard_map/ppermute | solution.py:348
  73.0 3.6 %shard_map.98 = (f32[7,8,128]{2,1,0:T(8,128)S(1)}, f32[7,8,128]{2,1,0:T(8,128)S(1)}, f32[7,8,128]{2,1,0:T(8,128)S(1)}, f32[7,8,128]{2,1,0:T(8,128)S(1)}, f32[7,8...) custom-call(s32[1]{0:T(128)} %bitcast.me_ref, ...), custom_call_target="tpu_custom_call" | custom-call | tf_op jit(solution)/shard_map/pallas_call | solution.py:260
  76.6 1.8 %collective-permute-start.23 = (f32[7,8,128]{2,1,0:T(8,128)S(1)}, f32[7,8,128]{2,1,0:T(8,128)S(1)}, u32[]{:S(2)}, u32[]{:S(2)}) collective-permute-start(f32[7,8,128]{2,1,0:T(8,128)S(1)} %get-tuple-element.35), channel_id=1, source_target_pairs={{0,32},{32,64},{64,96},{96,128},{128,160},{160,192},{192,224},{224... | collective-permute-start | bytes 86024 | tf_op jit(solution)/shard_map/ppermute | solution.py:272
  78.5 2.7 %collective-permute-start.24 = (f32[7,8,128]{2,1,0:T(8,128)S(1)}, f32[7,8,128]{2,1,0:T(8,128)S(1)}, u32[]{:S(2)}, u32[]{:S(2)}) collective-permute-start(f32[7,8,128]{2,1,0:T(8,128)S(1)} %get-tuple-element.36), channel_id=1, source_target_pairs={{0,64},{32,96},{64,128},{96,160},{128,192},{160,224},{192,0},{224,... | collective-permute-start | bytes 86024 | tf_op jit(solution)/shard_map/ppermute | solution.py:272
  82.3 3.6 %collective-permute-start.26 = (f32[7,8,128]{2,1,0:T(8,128)S(1)}, f32[7,8,128]{2,1,0:T(8,128)S(1)}, u32[]{:S(2)}, u32[]{:S(2)}) collective-permute-start(f32[7,8,128]{2,1,0:T(8,128)S(1)} %get-tuple-element.38), channel_id=1, source_target_pairs={{0,128},{32,160},{64,192},{96,224},{128,0},{160,32},{192,64},{224,... | collective-permute-start | bytes 86024 | tf_op jit(solution)/shard_map/ppermute | solution.py:272
  85.9 2.6 %collective-permute-start.27 = (f32[7,8,128]{2,1,0:T(8,128)S(1)}, f32[7,8,128]{2,1,0:T(8,128)S(1)}, u32[]{:S(2)}, u32[]{:S(2)}) collective-permute-start(f32[7,8,128]{2,1,0:T(8,128)S(1)} %get-tuple-element.39), channel_id=1, source_target_pairs={{0,160},{32,192},{64,224},{96,0},{128,32},{160,64},{192,96},{224,1... | collective-permute-start | bytes 86024 | tf_op jit(solution)/shard_map/ppermute | solution.py:272
  88.6 2.0 %collective-permute-start.28 = (f32[7,8,128]{2,1,0:T(8,128)S(1)}, f32[7,8,128]{2,1,0:T(8,128)S(1)}, u32[]{:S(2)}, u32[]{:S(2)}) collective-permute-start(f32[7,8,128]{2,1,0:T(8,128)S(1)} %get-tuple-element.40), channel_id=1, source_target_pairs={{0,192},{32,224},{64,0},{96,32},{128,64},{160,96},{192,128},{224,1... | collective-permute-start | bytes 86024 | tf_op jit(solution)/shard_map/ppermute | solution.py:272
  95.3 2.6 %collective-permute-start.31 = (f32[8,128]{1,0:T(8,128)S(1)}, f32[8,128]{1,0:T(8,128)S(1)}, u32[]{:S(2)}, u32[]{:S(2)}) collective-permute-start(f32[8,128]{1,0:T(8,128)S(1)} %fusion), channel_id=1, source_target_pairs={{0,2},{1,3},{2,0},{3,1},{4,6},{5,7},{6,4},{7,5},{8,10},{9,11},{10,... | collective-permute-start | bytes 12296 | tf_op jit(solution)/shard_map/ppermute | solution.py:294
  101.0 5.1 %collective-permute-done.33 = f32[8,128]{1,0:T(8,128)S(1)} collective-permute-done((f32[8,128]{1,0:T(8,128)S(1)}, f32[8,128]{1,0:T(8,128)S(1)}, u32[]{:S(2)}, u32[]{:S(2)}) %collective-permute-start.33) | collective-permute-done | bytes 4128 | tf_op jit(solution)/shard_map/ppermute | solution.py:294
  106.7 3.6 %collective-permute-start.35 = (f32[8,128]{1,0:T(8,128)S(1)}, f32[8,128]{1,0:T(8,128)S(1)}, u32[]{:S(2)}, u32[]{:S(2)}) collective-permute-start(f32[8,128]{1,0:T(8,128)S(1)} %add.99), channel_id=1, source_target_pairs={{0,16},{1,17},{2,18},{3,19},{4,20},{5,21},{6,22},{7,23},{8,24},{9,... | collective-permute-start | bytes 12296 | tf_op jit(solution)/shard_map/ppermute | solution.py:294
  111.9 3.2 %collective-permute-done.34 = f32[8,128]{1,0:T(8,128)S(1)} collective-permute-done((f32[8,128]{1,0:T(8,128)S(1)}, f32[8,128]{1,0:T(8,128)S(1)}, u32[]{:S(2)}, u32[]{:S(2)}) %collective-permute-start.34) | collective-permute-done | bytes 4128 | tf_op jit(solution)/shard_map/ppermute | solution.py:294
  (84 shorter events, 38.4 us)
Async XLA Ops:
  7.2 10.8 %collective-permute-start.10 = (f32[8,128]{1,0:T(8,128)S(1)}, f32[8,128]{1,0:T(8,128)S(1)}, u32[]{:S(2)}, u32[]{:S(2)}) collective-permute-start(f32[8,128]{1,0:T(8,128)S(1)} %add_add_fusion.2), channel_id=1, source_target_pairs={{0,4},{1,5},{2,6},{3,7},{4,0},{5,1},{6,2},{7,3},{8,12},{9,13},{10,... | collective-permute-start | bytes 12296 | tf_op jit(solution)/shard_map/ppermute | solution.py:294
  12.8 39.8 %collective-permute-start = (f32[14,16,128]{2,1,0:T(8,128)S(1)}, f32[14,16,128]{2,1,0:T(8,128)S(1)}, u32[]{:S(2)}, u32[]{:S(2)}) collective-permute-start(f32[14,16,128]{2,1,0:T(8,128)S(1)} %get-tuple-element.23), channel_id=1, source_target_pairs={{0,32},{32,64},{64,96},{96,128},{128,160},{160,192},{192,224},{224... | collective-permute-start | bytes 344072 | tf_op jit(solution)/shard_map/ppermute | solution.py:272
  14.7 39.5 %collective-permute-start.1 = (f32[14,16,128]{2,1,0:T(8,128)S(1)}, f32[14,16,128]{2,1,0:T(8,128)S(1)}, u32[]{:S(2)}, u32[]{:S(2)}) collective-permute-start(f32[14,16,128]{2,1,0:T(8,128)S(1)} %get-tuple-element.24), channel_id=1, source_target_pairs={{0,64},{32,96},{64,128},{96,160},{128,192},{160,224},{192,0},{224,... | collective-permute-start | bytes 344072 | tf_op jit(solution)/shard_map/ppermute | solution.py:272
  20.9 5.1 %collective-permute-start.12 = (f32[8,128]{1,0:T(8,128)S(1)}, f32[8,128]{1,0:T(8,128)S(1)}, u32[]{:S(2)}, u32[]{:S(2)}) collective-permute-start(f32[8,128]{1,0:T(8,128)S(1)} %add.83), channel_id=1, source_target_pairs={{0,16},{1,17},{2,18},{3,19},{4,20},{5,21},{6,22},{7,23},{8,24},{9,... | collective-permute-start | bytes 12296 | tf_op jit(solution)/shard_map/ppermute | solution.py:294
  27.1 7.8 %collective-permute-start.20 = (f32[8,128]{1,0:T(8,128)S(1)}, f32[8,128]{1,0:T(8,128)S(1)}, u32[]{:S(2)}, u32[]{:S(2)}) collective-permute-start(f32[8,128]{1,0:T(8,128)S(1)} %fusion.1.rest_0_.rest_8_), channel_id=1, source_target_pairs={{0,224},{32,0},{64,32},{96,64},{128,96},{160,128},{192,160},{224,1... | collective-permute-start | bytes 12296 | tf_op jit(solution)/shard_map/ppermute | solution.py:272
  28.5 7.4 %collective-permute-start.19 = (f32[8,128]{1,0:T(8,128)S(1)}, f32[8,128]{1,0:T(8,128)S(1)}, u32[]{:S(2)}, u32[]{:S(2)}) collective-permute-start(f32[8,128]{1,0:T(8,128)S(1)} %fusion.1.rest_0_.rest_8_), channel_id=1, source_target_pairs={{0,192},{32,224},{64,0},{96,32},{128,64},{160,96},{192,128},{224,1... | collective-permute-start | bytes 12296 | tf_op jit(solution)/shard_map/ppermute | solution.py:272
  30.8 8.3 %collective-permute-start.18 = (f32[8,128]{1,0:T(8,128)S(1)}, f32[8,128]{1,0:T(8,128)S(1)}, u32[]{:S(2)}, u32[]{:S(2)}) collective-permute-start(f32[8,128]{1,0:T(8,128)S(1)} %fusion.1.rest_0_.rest_8_), channel_id=1, source_target_pairs={{0,160},{32,192},{64,224},{96,0},{128,32},{160,64},{192,96},{224,1... | collective-permute-start | bytes 12296 | tf_op jit(solution)/shard_map/ppermute | solution.py:272
  34.9 7.7 %collective-permute-start.17 = (f32[8,128]{1,0:T(8,128)S(1)}, f32[8,128]{1,0:T(8,128)S(1)}, u32[]{:S(2)}, u32[]{:S(2)}) collective-permute-start(f32[8,128]{1,0:T(8,128)S(1)} %fusion.1.rest_0_.rest_8_), channel_id=1, source_target_pairs={{0,128},{32,160},{64,192},{96,224},{128,0},{160,32},{192,64},{224,... | collective-permute-start | bytes 12296 | tf_op jit(solution)/shard_map/ppermute | solution.py:272
  35.9 7.5 %collective-permute-start.16 = (f32[8,128]{1,0:T(8,128)S(1)}, f32[8,128]{1,0:T(8,128)S(1)}, u32[]{:S(2)}, u32[]{:S(2)}) collective-permute-start(f32[8,128]{1,0:T(8,128)S(1)} %fusion.1.rest_0_.rest_8_), channel_id=1, source_target_pairs={{0,96},{32,128},{64,160},{96,192},{128,224},{160,0},{192,32},{224,... | collective-permute-start | bytes 12296 | tf_op jit(solution)/shard_map/ppermute | solution.py:272
  39.1 5.7 %collective-permute-start.15 = (f32[8,128]{1,0:T(8,128)S(1)}, f32[8,128]{1,0:T(8,128)S(1)}, u32[]{:S(2)}, u32[]{:S(2)}) collective-permute-start(f32[8,128]{1,0:T(8,128)S(1)} %fusion.1.rest_0_.rest_8_), channel_id=1, source_target_pairs={{0,64},{32,96},{64,128},{96,160},{128,192},{160,224},{192,0},{224,... | collective-permute-start | bytes 12296 | tf_op jit(solution)/shard_map/ppermute | solution.py:272
  42.6 6.5 %collective-permute-start.14 = (f32[8,128]{1,0:T(8,128)S(1)}, f32[8,128]{1,0:T(8,128)S(1)}, u32[]{:S(2)}, u32[]{:S(2)}) collective-permute-start(f32[8,128]{1,0:T(8,128)S(1)} %fusion.1.rest_0_.rest_8_), channel_id=1, source_target_pairs={{0,32},{32,64},{64,96},{96,128},{128,160},{160,192},{192,224},{224... | collective-permute-start | bytes 12296 | tf_op jit(solution)/shard_map/ppermute | solution.py:272
  43.4 11.7 %collective-permute-start.2 = (f32[14,16,128]{2,1,0:T(8,128)S(1)}, f32[14,16,128]{2,1,0:T(8,128)S(1)}, u32[]{:S(2)}, u32[]{:S(2)}) collective-permute-start(f32[14,16,128]{2,1,0:T(8,128)S(1)} %get-tuple-element.25), channel_id=1, source_target_pairs={{0,96},{32,128},{64,160},{96,192},{128,224},{160,0},{192,32},{224,... | collective-permute-start | bytes 344072 | tf_op jit(solution)/shard_map/ppermute | solution.py:272
  44.9 10.2 %collective-permute-start.3 = (f32[14,16,128]{2,1,0:T(8,128)S(1)}, f32[14,16,128]{2,1,0:T(8,128)S(1)}, u32[]{:S(2)}, u32[]{:S(2)}) collective-permute-start(f32[14,16,128]{2,1,0:T(8,128)S(1)} %get-tuple-element.26), channel_id=1, source_target_pairs={{0,128},{32,160},{64,192},{96,224},{128,0},{160,32},{192,64},{224,... | collective-permute-start | bytes 344072 | tf_op jit(solution)/shard_map/ppermute | solution.py:272
  49.1 11.6 %collective-permute-start.4 = (f32[14,16,128]{2,1,0:T(8,128)S(1)}, f32[14,16,128]{2,1,0:T(8,128)S(1)}, u32[]{:S(2)}, u32[]{:S(2)}) collective-permute-start(f32[14,16,128]{2,1,0:T(8,128)S(1)} %get-tuple-element.27), channel_id=1, source_target_pairs={{0,160},{32,192},{64,224},{96,0},{128,32},{160,64},{192,96},{224,1... | collective-permute-start | bytes 344072 | tf_op jit(solution)/shard_map/ppermute | solution.py:272
  52.6 10.9 %collective-permute-start.5 = (f32[14,16,128]{2,1,0:T(8,128)S(1)}, f32[14,16,128]{2,1,0:T(8,128)S(1)}, u32[]{:S(2)}, u32[]{:S(2)}) collective-permute-start(f32[14,16,128]{2,1,0:T(8,128)S(1)} %get-tuple-element.28), channel_id=1, source_target_pairs={{0,192},{32,224},{64,0},{96,32},{128,64},{160,96},{192,128},{224,1... | collective-permute-start | bytes 344072 | tf_op jit(solution)/shard_map/ppermute | solution.py:272
  54.2 9.4 %collective-permute-start.6 = (f32[14,16,128]{2,1,0:T(8,128)S(1)}, f32[14,16,128]{2,1,0:T(8,128)S(1)}, u32[]{:S(2)}, u32[]{:S(2)}) collective-permute-start(f32[14,16,128]{2,1,0:T(8,128)S(1)} %get-tuple-element.29), channel_id=1, source_target_pairs={{0,224},{32,0},{64,32},{96,64},{128,96},{160,128},{192,160},{224,1... | collective-permute-start | bytes 344072 | tf_op jit(solution)/shard_map/ppermute | solution.py:272
  63.9 7.3 %collective-permute-start.21 = (f32[28,16,128]{2,1,0:T(8,128)S(1)}, f32[28,16,128]{2,1,0:T(8,128)S(1)}, u32[]{:S(2)}, u32[]{:S(2)}) collective-permute-start(f32[28,16,128]{2,1,0:T(8,128)S(1)} %get-tuple-element.31), channel_id=1, source_target_pairs={{0,1},{1,2},{2,3},{3,4},{4,5},{5,6},{6,7},{7,8},{8,9},{9,10},{10,1... | collective-permute-start | bytes 688136 | tf_op jit(solution)/shard_map/ppermute | solution.py:347
  65.9 7.2 %collective-permute-start.22 = (f32[28,16,128]{2,1,0:T(8,128)S(1)}, f32[28,16,128]{2,1,0:T(8,128)S(1)}, u32[]{:S(2)}, u32[]{:S(2)}) collective-permute-start(f32[28,16,128]{2,1,0:T(8,128)S(1)} %get-tuple-element.32), channel_id=1, source_target_pairs={{1,0},{2,1},{3,2},{4,3},{5,4},{6,5},{7,6},{8,7},{9,8},{10,9},{11,1... | collective-permute-start | bytes 688136 | tf_op jit(solution)/shard_map/ppermute | solution.py:348
  76.6 11.9 %collective-permute-start.23 = (f32[7,8,128]{2,1,0:T(8,128)S(1)}, f32[7,8,128]{2,1,0:T(8,128)S(1)}, u32[]{:S(2)}, u32[]{:S(2)}) collective-permute-start(f32[7,8,128]{2,1,0:T(8,128)S(1)} %get-tuple-element.35), channel_id=1, source_target_pairs={{0,32},{32,64},{64,96},{96,128},{128,160},{160,192},{192,224},{224... | collective-permute-start | bytes 86024 | tf_op jit(solution)/shard_map/ppermute | solution.py:272
  78.5 12.1 %collective-permute-start.24 = (f32[7,8,128]{2,1,0:T(8,128)S(1)}, f32[7,8,128]{2,1,0:T(8,128)S(1)}, u32[]{:S(2)}, u32[]{:S(2)}) collective-permute-start(f32[7,8,128]{2,1,0:T(8,128)S(1)} %get-tuple-element.36), channel_id=1, source_target_pairs={{0,64},{32,96},{64,128},{96,160},{128,192},{160,224},{192,0},{224,... | collective-permute-start | bytes 86024 | tf_op jit(solution)/shard_map/ppermute | solution.py:272
  81.2 10.6 %collective-permute-start.25 = (f32[7,8,128]{2,1,0:T(8,128)S(1)}, f32[7,8,128]{2,1,0:T(8,128)S(1)}, u32[]{:S(2)}, u32[]{:S(2)}) collective-permute-start(f32[7,8,128]{2,1,0:T(8,128)S(1)} %get-tuple-element.37), channel_id=1, source_target_pairs={{0,96},{32,128},{64,160},{96,192},{128,224},{160,0},{192,32},{224,... | collective-permute-start | bytes 86024 | tf_op jit(solution)/shard_map/ppermute | solution.py:272
  82.3 9.5 %collective-permute-start.26 = (f32[7,8,128]{2,1,0:T(8,128)S(1)}, f32[7,8,128]{2,1,0:T(8,128)S(1)}, u32[]{:S(2)}, u32[]{:S(2)}) collective-permute-start(f32[7,8,128]{2,1,0:T(8,128)S(1)} %get-tuple-element.38), channel_id=1, source_target_pairs={{0,128},{32,160},{64,192},{96,224},{128,0},{160,32},{192,64},{224,... | collective-permute-start | bytes 86024 | tf_op jit(solution)/shard_map/ppermute | solution.py:272
  85.9 5.9 %collective-permute-start.27 = (f32[7,8,128]{2,1,0:T(8,128)S(1)}, f32[7,8,128]{2,1,0:T(8,128)S(1)}, u32[]{:S(2)}, u32[]{:S(2)}) collective-permute-start(f32[7,8,128]{2,1,0:T(8,128)S(1)} %get-tuple-element.39), channel_id=1, source_target_pairs={{0,160},{32,192},{64,224},{96,0},{128,32},{160,64},{192,96},{224,1... | collective-permute-start | bytes 86024 | tf_op jit(solution)/shard_map/ppermute | solution.py:272
  106.7 5.2 %collective-permute-start.35 = (f32[8,128]{1,0:T(8,128)S(1)}, f32[8,128]{1,0:T(8,128)S(1)}, u32[]{:S(2)}, u32[]{:S(2)}) collective-permute-start(f32[8,128]{1,0:T(8,128)S(1)} %add.99), channel_id=1, source_target_pairs={{0,16},{1,17},{2,18},{3,19},{4,20},{5,21},{6,22},{7,23},{8,24},{9,... | collective-permute-start | bytes 12296 | tf_op jit(solution)/shard_map/ppermute | solution.py:294
  (21 other events, 75.0 us)

commit v2 on v1

v2 whole, which is shorter than its diff:
```python
import functools

import jax
import jax.numpy as jnp
from jax import lax
from jax.experimental import pallas as pl
from jax.experimental.pallas import tpu as pltpu
from jax.sharding import PartitionSpec as P

F32 = jnp.float32
BF16 = jnp.bfloat16
PLANES = 8
LINES = 64
ZC = 16
PAIRS = 14
STRIP = 16
WELL_ROW = 3
VMEM_LIMIT = 24 * 1024 * 1024

VMEM = pl.BlockSpec(memory_space=pltpu.VMEM)


def split3(x):
    hi = x.astype(BF16).astype(F32)
    rest = x - hi
    mid = rest.astype(BF16).astype(F32)
    lo = rest - mid
    return hi, mid, lo


def split_rows(x):
    return jnp.concatenate(split3(x), axis=0).astype(BF16)


def join_rows(y, rows):
    return y[0:rows] + y[rows : 2 * rows] + y[2 * rows : 3 * rows]


def lane_iota(rows):
    return lax.broadcasted_iota(jnp.int32, (rows, 128), 1)


def row_iota(rows):
    return lax.broadcasted_iota(jnp.int32, (rows, 128), 0)


def roll_lanes(x, shift):
    shift %= 128
    return x if shift == 0 else pltpu.roll(x, shift, 1)


def wells_kernel(wells, out, wide):
    held = wells.shape[1]
    wide[...] = jnp.zeros_like(wide)
    wide[0:3, 0:held] = wells[...]
    row = jnp.zeros((1, 128), F32)
    for c in range(3):
        row = row + roll_lanes(wide[c : c + 1], WELL_ROW + held * c)
    out[...] = jnp.broadcast_to(row, out.shape)


def pack_kernel(rhs, einv, xc, yc, cell, well, weight, wells, *rest):
    out, rhs_v, einv_v, xc_v, yc_v, cell_v, well_v, weight_v, wells_v, turned, sems = rest
    moves = [
        pltpu.make_async_copy(src, dst, sems.at[i])
        for i, (src, dst) in enumerate(
            [
                (rhs, rhs_v),
                (einv, einv_v),
                (xc, xc_v),
                (yc, yc_v),
                (cell, cell_v),
                (well, well_v),
                (weight, weight_v),
                (wells, wells_v),
            ]
        )
    ]
    for move in moves:
        move.start()
    arrays = (
        [(rhs_v, 0, i) for i in range(6)]
        + [(einv_v, 1, i) for i in range(9)]
        + [(xc_v, 2, i) for i in range(6)]
        + [(yc_v, 3, i) for i in range(6)]
    )
    waited = -1
    for g in range(PAIRS):
        ends = []
        for n in (2 * g, 2 * g + 1):
            if n == 27:
                ends.append(jnp.zeros((LINES, 128), F32))
                continue
            ref, stage, i = arrays[n]
            if stage > waited:
                moves[stage].wait()
                waited = stage
            ends.append(ref[i])
        turned[g] = jnp.concatenate(ends, axis=0).T
    for stage in (4, 5, 6, 7):
        moves[stage].wait()
    perfs = jnp.concatenate(
        [cell_v[...].astype(F32), well_v[...].astype(F32), weight_v[...], jnp.zeros((ZC - 3, LINES), F32)], axis=0
    )
    lines = wells_v.shape[0]
    gathered = jnp.concatenate([wells_v[...], jnp.zeros((128 - lines, 128), F32)], axis=0).T[0:ZC]
    perfs = jnp.concatenate([jnp.zeros((ZC, 64), F32), perfs], axis=1) + roll_lanes(gathered, 64)
    low = lane_iota(ZC) < 64
    for t in range(PLANES):
        rows = slice(ZC * t, ZC * t + ZC)
        for g in range(PAIRS - 1):
            out[t, g] = turned[g, rows, :]
        out[t, PAIRS - 1] = jnp.where(low, turned[PAIRS - 1, rows, :], perfs)


def perf_tiles(chunks):
    low = lane_iota(8) < 64
    last = PAIRS - 1
    return [
        jnp.where(low, roll_lanes(chunks[2 * j, last, 0:8], 64), chunks[2 * j + 1, last, 0:8])
        for j in range(PLANES // 2)
    ]


def ints(row):
    return row.astype(jnp.int32)


def place_of(tile, first_z):
    cell = ints(tile[0:1])
    at_z = (cell & 127) == row_iota(ZC) + first_z
    at_y = jnp.where(((cell >> 7) & 63) == row_iota(128), 1.0, 0.0).astype(BF16)
    return at_z, at_y


def sides(at_z):
    low = lane_iota(ZC) < 64
    return [jnp.logical_and(at_z, low), jnp.logical_and(at_z, jnp.logical_not(low))]


def strip_kernel(line_bits, held, chunks, first_ref, last_ref, src_ref):
    bits = held.bit_length() - 1
    lines = 1 << line_bits
    me = lax.axis_index("gx")
    tiles = perf_tiles(chunks)
    place = lane_iota(ZC) >> 5
    wells = []
    for u in range(2):
        tile = None
        for v in range(4):
            part = roll_lanes(chunks[4 * u + v, PAIRS - 1], 32 * v - 64)
            tile = part if v == 0 else jnp.where(place == v, part, tile)
        wells.append(tile)
    wells = split_rows(jnp.concatenate(wells, axis=1))
    low = lane_iota(ZC) < 64
    for j in range(PLANES // 2):
        well = ints(tiles[j][1:2])
        owner = well >> bits
        at = (owner >> line_bits) * 32 + (owner & (lines - 1))
        hot = jnp.where(at == row_iota(256), 1.0, 0.0).astype(BF16)
        picked = join_rows(jnp.dot(wells, hot, preferred_element_type=F32), ZC)
        terms = []
        for c in range(3):
            term = jnp.zeros((1, 128), F32)
            for i in range(held):
                term = jnp.where((well & (held - 1)) == i, picked[WELL_ROW + held * c + i : WELL_ROW + held * c + i + 1], term)
            terms.append(term * tiles[j][2:3])
        at_z, at_y = place_of(tiles[j], me * ZC)
        rows = [jnp.where(keep, term, 0.0) for keep in sides(at_z) for term in terms]
        left = split_rows(jnp.concatenate(rows, axis=0))
        spread = lax.dot_general(left, at_y, (((1,), (1,)), ((), ())), preferred_element_type=F32)
        spread = join_rows(spread, 96)
        for side in range(2):
            c0, c1, c2 = (spread[48 * side + 16 * c : 48 * side + 16 * c + 16] for c in range(3))
            d = 2 * j + side
            src_ref[d, 0] = jnp.where(low, c0, roll_lanes(c1, 64))
            src_ref[d, 1] = jnp.where(low, c2, roll_lanes(c0, 64))
            src_ref[d, 2] = jnp.where(low, c1, roll_lanes(c2, 64))
    slot = (lane_iota(ZC) & 63) >> 4
    for q in range(PLANES * PAIRS // 4):
        first = last = None
        for s in range(4):
            d, g = divmod(4 * q + s, PAIRS)
            x = chunks[d, g]
            if g < 3:
                x = x + src_ref[d, g]
            a = roll_lanes(x, 16 * s)
            b = roll_lanes(x, 16 * s + 80)
            first = a if s == 0 else jnp.where(slot == s, a, first)
            last = b if s == 0 else jnp.where(slot == s, b, last)
        first_ref[q] = first
        last_ref[q] = last


def block_apply(blocks, v):
    return [blocks[3 * a] * v[0] + blocks[3 * a + 1] * v[1] + blocks[3 * a + 2] * v[2] for a in range(3)]


def plane_apply(blocks, lower, upper, v):
    w = block_apply(blocks, v)
    u = [v[c] - lower[c] * roll_lanes(w[c], 1) - upper[c] * roll_lanes(w[c], 127) for c in range(3)]
    return block_apply(blocks, u)


def march_kernel(share, chunks, src, before, after, out_ref, grid, field):
    me = lax.axis_index("gx")
    lane = lane_iota(ZC)
    own = lane < 64
    right = lane < 80
    left = lane >= 112

    for d in range(PLANES):
        for g in range(PAIRS):
            q, s = divmod(PAIRS * d + g, 4)
            x = chunks[d, g]
            if g < 3:
                x = x + src[d, g]
            for h in range(2):
                n = 2 * g + h
                if n == 27:
                    continue
                at = 16 * s + 64 * h
                edge = jnp.where(right, roll_lanes(after[q], 64 - at), roll_lanes(before[q], 112 - at))
                edge = jnp.where(jnp.logical_or(right, left), edge, 0.0)
                grid[d, n] = jnp.where(own, roll_lanes(x, 64 * h), edge)

    for t in range(2):
        rows = slice(8 * t, 8 * t + 8)
        state = None
        for i in range(PLANES):
            blocks = [grid[i, 6 + n, rows] for n in range(9)]
            lower = [grid[i, 21 + c, rows] for c in range(3)]
            upper = [grid[i, 24 + c, rows] for c in range(3)]
            new = []
            for k in range(2):
                v = [grid[i, 3 * k + c, rows] for c in range(3)]
                if i > 0:
                    v = [v[c] - grid[i, 15 + c, rows] * state[k][c] for c in range(3)]
                new.append(plane_apply(blocks, lower, upper, v))
            state = new
            for k in range(2):
                for c in range(3):
                    field[i, 3 * k + c, rows] = state[k][c]
        for i in range(PLANES - 2, -1, -1):
            blocks = [grid[i, 6 + n, rows] for n in range(9)]
            lower = [grid[i, 21 + c, rows] for c in range(3)]
            upper = [grid[i, 24 + c, rows] for c in range(3)]
            new = []
            for k in range(2):
                v = [grid[i, 18 + c, rows] * state[k][c] for c in range(3)]
                p = plane_apply(blocks, lower, upper, v)
                new.append([field[i, 3 * k + c, rows] - p[c] for c in range(3)])
            state = new
            for k in range(2):
                for c in range(3):
                    field[i, 3 * k + c, rows] = state[k][c]

    for i in range(PLANES):
        for c in range(3):
            pair = jnp.where(own, field[i, c], roll_lanes(field[i, 3 + c], 64))
            out_ref[i, 2 * c] = pair[0:8]
            out_ref[i, 2 * c + 1] = pair[8:16]

    tiles = perf_tiles(chunks)
    parts = []
    for j in range(PLANES // 2):
        at_z, at_y = place_of(tiles[j], me * ZC)
        found = None
        for side, keep in enumerate(sides(at_z)):
            x = jnp.concatenate([field[2 * j + side, 3 + c] for c in range(3)], axis=0)
            got = join_rows(jnp.dot(split_rows(x), at_y, preferred_element_type=F32), 48)
            got = [jnp.where(keep, got[16 * c : 16 * c + 16], 0.0) for c in range(3)]
            found = got if found is None else [a + b for a, b in zip(found, got)]
        value = [jnp.sum(f, axis=0, keepdims=True) * tiles[j][2:3] for f in found]
        value = jnp.concatenate(value + [jnp.zeros((5, 128), F32)], axis=0)
        parts.append(jnp.concatenate(list(split3(value)) + [jnp.zeros((8, 128), F32)], axis=0).astype(BF16))
    wells = [ints(tile[1:2]) for tile in tiles]
    row = row_iota(128)
    for i in range(PLANES):
        total = jnp.zeros((32, 128), F32)
        for j in range(PLANES // 2):
            hot = jnp.where(wells[j] == row + share * i, 1.0, 0.0).astype(BF16)
            total += lax.dot_general(parts[j], hot, (((1,), (1,)), ((), ())), preferred_element_type=F32)
        out_ref[i, 6] = join_rows(total, 8)


def unpack_kernel(chunks, out, sums, turned):
    total = chunks[0, 6]
    for t in range(1, PLANES):
        total = total + chunks[t, 6]
    sums[...] = jnp.broadcast_to(total[None], sums.shape)
    for t in range(PLANES):
        for c in range(3):
            for h in range(2):
                turned[c, ZC * t + 8 * h : ZC * t + 8 * h + 8] = chunks[t, 2 * c + h]
    for c in range(3):
        y = turned[c].T
        out[0, c] = y[0:LINES]
        out[1, c] = y[LINES : 2 * LINES]


def final_kernel(sums, out):
    held = out.shape[1]
    total = sums[0]
    for b in range(1, sums.shape[0]):
        total = total + sums[b]
    shift = (128 - held * lax.axis_index("gy")) & 127
    out[...] = pltpu.roll(total, shift, 1)[0:3, 0:held]


def call(kernel, inputs, out_shape, scratch=(), space=VMEM):
    if space is not VMEM:
        inputs = [pltpu.with_memory_space_constraint(x, space) for x in inputs]
        space = pl.BlockSpec(memory_space=space)
    return pl.pallas_call(
        kernel,
        out_shape=out_shape,
        in_specs=[space] * len(inputs),
        out_specs=jax.tree.map(lambda _: VMEM, out_shape),
        scratch_shapes=list(scratch),
        compiler_params=pltpu.CompilerParams(vmem_limit_bytes=VMEM_LIMIT),
    )(*inputs)


def shape(*dims):
    return jax.ShapeDtypeStruct(dims, F32)


def per_device(
    adjoint_rhs, block_inverse, x_couplings, y_couplings, perf_cell, perf_well, perf_weight, well_adjoint
):
    held = well_adjoint.shape[1]
    lines = lax.axis_size("gy")
    perfs = perf_cell.shape[0]

    row = call(wells_kernel, [well_adjoint], shape(lines, 128), [pltpu.VMEM((8, 128), F32)])
    wells = lax.all_to_all(row, "gy", 0, 0, tiled=True)

    packed = call(
        pack_kernel,
        [
            adjoint_rhs.reshape(6, LINES, 128),
            block_inverse.reshape(9, LINES, 128),
            x_couplings.reshape(6, LINES, 128),
            y_couplings.reshape(6, LINES, 128),
            perf_cell.reshape(1, perfs),
            perf_well.reshape(1, perfs),
            perf_weight.reshape(1, perfs),
            wells,
        ],
        shape(PLANES, PAIRS, ZC, 128),
        [
            pltpu.VMEM((6, LINES, 128), F32),
            pltpu.VMEM((9, LINES, 128), F32),
            pltpu.VMEM((6, LINES, 128), F32),
            pltpu.VMEM((6, LINES, 128), F32),
            pltpu.VMEM((1, perfs), jnp.int32),
            pltpu.VMEM((1, perfs), jnp.int32),
            pltpu.VMEM((1, perfs), F32),
            pltpu.VMEM((lines, 128), F32),
            pltpu.VMEM((PAIRS, 128, 128), F32),
            pltpu.SemaphoreType.DMA((8,)),
        ],
        space=pltpu.HBM,
    )
    chunks = lax.all_to_all(packed, "gx", 0, 0)

    strip = shape(PLANES * PAIRS // 4, ZC, 128)
    first, last, src = call(
        functools.partial(strip_kernel, lines.bit_length() - 1, held),
        [chunks],
        [strip, strip, shape(PLANES, 3, ZC, 128)],
    )
    up = [(i, i + 1) for i in range(lines - 1)]
    before = lax.ppermute(last, "gy", up)
    after = lax.ppermute(first, "gy", [(j, i) for i, j in up])

    back = call(
        functools.partial(march_kernel, held * lines),
        [chunks, src, before, after],
        shape(PLANES, 7, 8, 128),
        [pltpu.VMEM((PLANES, 27, ZC, 128), F32), pltpu.VMEM((PLANES, 6, ZC, 128), F32)],
    )
    got = lax.all_to_all(back, "gx", 0, 0)
    precond, sums = call(
        unpack_kernel,
        [got],
        [shape(2, 3, LINES, 128), shape(lines, 8, 128)],
        [pltpu.VMEM((3, 128, 128), F32)],
    )
    sums = lax.all_to_all(sums, "gy", 0, 0)
    well_update = call(final_kernel, [sums], shape(3, held))
    return precond.reshape(adjoint_rhs.shape), well_update


def solution(mesh):
    placed = (
        P(None, None, "gx", "gy", None),
        P(None, None, "gx", "gy", None),
        P(None, None, "gx", "gy", None),
        P(None, None, "gx", "gy", None),
        P(("gx", "gy")),
        P(("gx", "gy")),
        P(("gx", "gy")),
        P(None, ("gx", "gy")),
    )
    return jax.shard_map(
        per_device,
        mesh=mesh,
        in_specs=placed,
        out_specs=(P(None, None, "gx", "gy", None), P(None, ("gx", "gy"))),
        check_vma=False,
    )
```

time: 116 us -> 95.3 us (0.82)
  the two profiles are of different devices: /device:TPU:6 before, /device:TPU:1 now
where the time goes in v2:
time: 95.3 us; the launch traced here: 95 us
  blocking collectives  74.4 us (78%)
  Pallas kernels  7.47 us (8%)
  starting transfers between devices  6.36 us (7%)
  waiting for transfers between devices  5.41 us (6%)
    all_to_all x1, blocking collectives, per_device(): chunks = lax.all_to_all(packed, 'gx', 0, 0)  32.7 us
    all_to_all x1, blocking collectives, per_device(): wells = lax.all_to_all(row, 'gy', 0, 0, tiled=True)  15.3 us
    all_to_all x1, blocking collectives, per_device(): sums = lax.all_to_all(sums, 'gy', 0, 0)  15.1 us
    all_to_all x1, blocking collectives, per_device(): got = lax.all_to_all(back, 'gx', 0, 0)  11.4 us
    pallas_call x6, Pallas kernels, call(): pl.pallas_call(kernel, out_shape=out_shape, in_specs=[space] * len(inputs...  7.47 us
    ppermute x1, starting transfers between devices, per_device(): before = lax.ppermute(last, 'gy', up)  4.44 us
    ppermute x1, waiting for transfers between devices, per_device(): after = lax.ppermute(first, 'gy', [(j, i) for i, j in up])  4.4 us
    ppermute x1, starting transfers between devices, per_device(): after = lax.ppermute(first, 'gy', [(j, i) for i, j in up])  1.92 us
  transfers between devices with their start and end apart: 2, of which 2 were waited for; matrix products, arithmetic and copies ran while one was open for 0% of the time, Pallas kernels for 0%

profile of v2, /device:TPU:1, one launch (start us, length us, event | category | flops | bytes accessed | tf_op | source)
XLA Modules:
  0.0 95.0 jit_solution(13569572008895903211)
XLA Ops:
  0.6 0.0 copy-start
  0.6 0.7 copy-done
  1.3 0.1 shard_map.95
  1.4 15.3 %all_to_all.26 = f32[32,1,128]{2,1,0:T(1,128)} all-to-all(f32[32,1,128]{2,1,0:T(1,128)S(1)} %bitcast.14), channel_id=1, replica_groups=mesh['gx'=8,'gy'=32] {'gy'}, dimensions={0} | all-to-all | bytes 32768 | tf_op jit(solution)/shard_map/all_to_all | solution.py:337
  16.7 1.7 %shard_map.96 = f32[8,14,16,128]{3,2,1,0:T(8,128)S(1)} custom-call(f32[6,64,128]{2,1,0:T(8,128)} %bitcast.16, f32[9,64,128]{2,1,0:T(8,128)} %bitcast.15, f32[6,64,128]{2,1,0:T(8,128)} %bitcast.17, f32[6,64,128]{2,1,0:T(8,128)} %bitcast.18, s32[1,64]{1,0:T(1,128)} %bitcast.20, s32[1,64]{1,0:T(1,128)} %bitcast.21, f32[1,64]{1,0:T(1,128)} %bitcast.22, ...), custom_call_target="tpu_custom_call" | custom-call | tf_op jit(solution)/shard_map/pallas_call | solution.py:315
  18.4 32.7 %all_to_all.27.chunks = f32[8,14,16,128]{3,2,1,0:T(8,128)S(1)} all-to-all(f32[8,14,16,128]{3,2,1,0:T(8,128)S(1)} %shard_map.96), channel_id=1, replica_groups=mesh['gx'=8,'gy'=32] {'gx'}, dimensions={0} | all-to-all | bytes 1835008 | tf_op jit(solution)/shard_map/all_to_all | solution.py:366
  51.1 0.7 shard_map.97
  51.8 4.4 %collective-permute-start = (f32[28,16,128]{2,1,0:T(8,128)S(1)}, f32[28,16,128]{2,1,0:T(8,128)S(1)}, u32[]{:S(2)}, u32[]{:S(2)}) collective-permute-start(f32[28,16,128]{2,1,0:T(8,128)S(1)} %get-tuple-element.8), channel_id=1, source_target_pairs={{0,1},{1,2},{2,3},{3,4},{4,5},{5,6},{6,7},{7,8},{8,9},{9,10},{10,1... | collective-permute-start | bytes 688136 | tf_op jit(solution)/shard_map/ppermute | solution.py:375
  56.3 1.9 %collective-permute-start.1 = (f32[28,16,128]{2,1,0:T(8,128)S(1)}, f32[28,16,128]{2,1,0:T(8,128)S(1)}, u32[]{:S(2)}, u32[]{:S(2)}) collective-permute-start(f32[28,16,128]{2,1,0:T(8,128)S(1)} %get-tuple-element.9), channel_id=1, source_target_pairs={{1,0},{2,1},{3,2},{4,3},{5,4},{6,5},{7,6},{8,7},{9,8},{10,9},{11,1... | collective-permute-start | bytes 688136 | tf_op jit(solution)/shard_map/ppermute | solution.py:376
  58.2 1.0 %collective-permute-done.before = f32[28,16,128]{2,1,0:T(8,128)S(1)} collective-permute-done((f32[28,16,128]{2,1,0:T(8,128)S(1)}, f32[28,16,128]{2,1,0:T(8,128)S(1)}, u32[]{:S(2)}, u32[]{:S(2)}) %collective-permute-start) | collective-permute-done | bytes 229408 | tf_op jit(solution)/shard_map/ppermute | solution.py:375
  59.2 4.4 %collective-permute-done.1.after = f32[28,16,128]{2,1,0:T(8,128)S(1)} collective-permute-done((f32[28,16,128]{2,1,0:T(8,128)S(1)}, f32[28,16,128]{2,1,0:T(8,128)S(1)}, u32[]{:S(2)}, u32[]{:S(2)}) %collective-permute-start.1) | collective-permute-done | bytes 229408 | tf_op jit(solution)/shard_map/ppermute | solution.py:376
  63.6 3.4 %shard_map.98 = f32[8,7,8,128]{3,2,1,0:T(8,128)S(1)} custom-call(f32[8,14,16,128]{3,2,1,0:T(8,128)S(1)} %all_to_all.27.chunks, f32[8,3,16,128]{3,2,1,0:T(8,128)S(1)} %get-tuple-element.7.src, f32[28,16,128]{2,1,0:T(8,128)S(1)} %collective-permute-done.before, f32[28,16,128]{2,1,0:T(8,128)S(1)} %collective-permute-done.1.after), custom_call_target="tpu_custom_call" | custom-call | tf_op jit(solution)/shard_map/pallas_call | solution.py:315
  67.1 11.4 %all_to_all.28.chunks = f32[8,7,8,128]{3,2,1,0:T(8,128)S(1)} all-to-all(f32[8,7,8,128]{3,2,1,0:T(8,128)S(1)} %shard_map.98), channel_id=1, replica_groups=mesh['gx'=8,'gy'=32] {'gx'}, dimensions={0} | all-to-all | bytes 458752 | tf_op jit(solution)/shard_map/all_to_all | solution.py:384
  78.5 0.8 shard_map.99
  79.3 15.1 %all_to_all.29.sums = f32[32,8,128]{2,1,0:T(8,128)S(1)} all-to-all(f32[32,8,128]{2,1,0:T(8,128)S(1)} %get-tuple-element.11), channel_id=1, replica_groups=mesh['gx'=8,'gy'=32] {'gy'}, dimensions={0} | all-to-all | bytes 262144 | tf_op jit(solution)/shard_map/all_to_all | solution.py:391
  94.3 0.7 shard_map.100
Async XLA Ops:
  0.6 0.7 copy-start
  51.8 7.4 %collective-permute-start = (f32[28,16,128]{2,1,0:T(8,128)S(1)}, f32[28,16,128]{2,1,0:T(8,128)S(1)}, u32[]{:S(2)}, u32[]{:S(2)}) collective-permute-start(f32[28,16,128]{2,1,0:T(8,128)S(1)} %get-tuple-element.8), channel_id=1, source_target_pairs={{0,1},{1,2},{2,3},{3,4},{4,5},{5,6},{6,7},{7,8},{8,9},{9,10},{10,1... | collective-permute-start | bytes 688136 | tf_op jit(solution)/shard_map/ppermute | solution.py:375
  56.3 7.3 %collective-permute-start.1 = (f32[28,16,128]{2,1,0:T(8,128)S(1)}, f32[28,16,128]{2,1,0:T(8,128)S(1)}, u32[]{:S(2)}, u32[]{:S(2)}) collective-permute-start(f32[28,16,128]{2,1,0:T(8,128)S(1)} %get-tuple-element.9), channel_id=1, source_target_pairs={{1,0},{2,1},{3,2},{4,3},{5,4},{6,5},{7,6},{8,7},{9,8},{10,9},{11,1... | collective-permute-start | bytes 688136 | tf_op jit(solution)/shard_map/ppermute | solution.py:376

commit v3 on v2

v3 whole, which is shorter than its diff:
```python
import functools

import jax
import jax.numpy as jnp
from jax import lax
from jax.experimental import pallas as pl
from jax.experimental.pallas import tpu as pltpu
from jax.sharding import PartitionSpec as P

F32 = jnp.float32
BF16 = jnp.bfloat16
PLANES = 8
LINES = 64
ZC = 16
PAIRS = 14
STRIP = 16
WELL_ROW = 3
STRIPS = PLANES * PAIRS // 4
VMEM_LIMIT = 24 * 1024 * 1024

VMEM = pl.BlockSpec(memory_space=pltpu.VMEM)


def split3(x):
    hi = x.astype(BF16).astype(F32)
    rest = x - hi
    mid = rest.astype(BF16).astype(F32)
    lo = rest - mid
    return hi, mid, lo


def split_rows(x):
    return jnp.concatenate(split3(x), axis=0).astype(BF16)


def join_rows(y, rows):
    return y[0:rows] + y[rows : 2 * rows] + y[2 * rows : 3 * rows]


def lane_iota(rows):
    return lax.broadcasted_iota(jnp.int32, (rows, 128), 1)


def row_iota(rows):
    return lax.broadcasted_iota(jnp.int32, (rows, 128), 0)


def roll_lanes(x, shift):
    shift %= 128
    return x if shift == 0 else pltpu.roll(x, shift, 1)


def pack_kernel(rhs, einv, xc, yc, cell, well, weight, wells, *rest):
    out, rhs_v, einv_v, xc_v, yc_v, cell_v, well_v, weight_v, wells_v, wide, turned, sems = rest
    moves = [
        pltpu.make_async_copy(src, dst, sems.at[i])
        for i, (src, dst) in enumerate(
            [
                (rhs, rhs_v),
                (einv, einv_v),
                (xc, xc_v),
                (yc, yc_v),
                (cell, cell_v),
                (well, well_v),
                (weight, weight_v),
                (wells, wells_v),
            ]
        )
    ]
    for move in moves:
        move.start()
    arrays = (
        [(rhs_v, 0, i) for i in range(6)]
        + [(einv_v, 1, i) for i in range(9)]
        + [(xc_v, 2, i) for i in range(6)]
        + [(yc_v, 3, i) for i in range(6)]
    )
    waited = -1
    for g in range(PAIRS):
        ends = []
        for n in (2 * g, 2 * g + 1):
            if n == 27:
                ends.append(jnp.zeros((LINES, 128), F32))
                continue
            ref, stage, i = arrays[n]
            if stage > waited:
                moves[stage].wait()
                waited = stage
            ends.append(ref[i])
        turned[g] = jnp.concatenate(ends, axis=0).T
    for stage in (4, 5, 6, 7):
        moves[stage].wait()
    held = wells_v.shape[1]
    wide[...] = jnp.zeros_like(wide)
    wide[0, 0:LINES] = cell_v[0].astype(F32)
    wide[1, 0:LINES] = well_v[0].astype(F32)
    wide[2, 0:LINES] = weight_v[0]
    wide[8:11, 0:held] = wells_v[...]
    own = wide[8:9] + roll_lanes(wide[9:10], held) + roll_lanes(wide[10:11], 2 * held)
    wide[8:11] = jnp.zeros((3, 128), F32)
    wide[WELL_ROW : WELL_ROW + 1] = own
    perfs = roll_lanes(wide[...], 64)
    low = lane_iota(ZC) < 64
    for t in range(PLANES):
        rows = slice(ZC * t, ZC * t + ZC)
        for g in range(PAIRS - 1):
            out[t, g] = turned[g, rows, :]
        out[t, PAIRS - 1] = jnp.where(low, turned[PAIRS - 1, rows, :], perfs)


def perf_tiles(chunks):
    low = lane_iota(8) < 64
    last = PAIRS - 1
    return [
        jnp.where(low, roll_lanes(chunks[2 * j, last, 0:8], 64), chunks[2 * j + 1, last, 0:8])
        for j in range(PLANES // 2)
    ]


def ints(row):
    return row.astype(jnp.int32)


def place_of(tile, first_z):
    cell = ints(tile[0:1])
    at_z = (cell & 127) == row_iota(ZC) + first_z
    at_y = jnp.where(((cell >> 7) & 63) == row_iota(128), 1.0, 0.0).astype(BF16)
    return at_z, at_y


def on_even():
    return jnp.zeros((ZC, 128), jnp.int32) + (lax.axis_index("gy") & 1) == 0


def sides(at_z):
    low = lane_iota(ZC) < 64
    return [jnp.logical_and(at_z, low), jnp.logical_and(at_z, jnp.logical_not(low))]


def strip_kernel(chunks, near_ref, far_ref, wells_ref):
    last = PAIRS - 1
    own = jnp.concatenate([chunks[d, last, WELL_ROW : WELL_ROW + 1] for d in range(PLANES)], axis=0)
    wells_ref[...] = jnp.broadcast_to(roll_lanes(own, 64)[None], wells_ref.shape)
    tiles = perf_tiles(chunks)
    for u in range(2):
        pair = jnp.concatenate([tiles[2 * u], tiles[2 * u + 1]], axis=0)
        near_ref[STRIPS + u] = pair
        far_ref[STRIPS + u] = pair
    slot = (lane_iota(ZC) & 63) >> 4
    even = on_even()
    for q in range(PLANES * PAIRS // 4):
        first = last = None
        for s in range(4):
            d, g = divmod(4 * q + s, PAIRS)
            x = chunks[d, g]
            a = roll_lanes(x, 16 * s)
            b = roll_lanes(x, 16 * s + 80)
            first = a if s == 0 else jnp.where(slot == s, a, first)
            last = b if s == 0 else jnp.where(slot == s, b, last)
        near_ref[q] = jnp.where(even, last, first)
        far_ref[q] = jnp.where(even, first, last)


def block_apply(blocks, v):
    return [blocks[3 * a] * v[0] + blocks[3 * a + 1] * v[1] + blocks[3 * a + 2] * v[2] for a in range(3)]


def plane_apply(blocks, lower, upper, v):
    w = block_apply(blocks, v)
    u = [v[c] - lower[c] * roll_lanes(w[c], 1) - upper[c] * roll_lanes(w[c], 127) for c in range(3)]
    return block_apply(blocks, u)


def sources(line_bits, bits, chunks, wells_ref, near, far, src):
    held = 1 << bits
    first_z = lax.axis_index("gx") * ZC
    wells = split_rows(wells_ref[...].reshape(-1, 128).T[0:ZC])
    own = perf_tiles(chunks)
    row = row_iota(128)
    odd = lax.axis_index("gy") & 1
    start = [64 + 48 * odd, 112 - 48 * odd]
    spans = [row < 64] + [jnp.logical_and(row >= first, row < first + 16) for first in start]
    for j in range(PLANES // 2):
        half = slice(8 * (j % 2), 8 * (j % 2) + 8)
        total = None
        for tile, span, base in zip([own[j], near[STRIPS + j // 2, half], far[STRIPS + j // 2, half]], spans, (0, 64, 64)):
            well = ints(tile[1:2])
            owner = well >> bits
            at = (owner & ((1 << line_bits) - 1)) * PLANES + (owner >> line_bits)
            hot = jnp.where(at == row_iota(wells.shape[1]), 1.0, 0.0).astype(BF16)
            picked = join_rows(jnp.dot(wells, hot, preferred_element_type=F32), ZC)
            terms = []
            for c in range(3):
                term = jnp.zeros((1, 128), F32)
                for i in range(held):
                    term = jnp.where((well & (held - 1)) == i, picked[held * c + i : held * c + i + 1], term)
                terms.append(term * tile[2:3])
            cell = ints(tile[0:1])
            at_z = (cell & 127) == row_iota(ZC) + first_z
            at_y = ((cell >> 7) & 63) + base == row
            at_y = jnp.where(jnp.logical_and(at_y, span), 1.0, 0.0).astype(BF16)
            rows = [jnp.where(keep, term, 0.0) for keep in sides(at_z) for term in terms]
            rows = split_rows(jnp.concatenate(rows, axis=0))
            spread = lax.dot_general(rows, at_y, (((1,), (1,)), ((), ())), preferred_element_type=F32)
            total = spread if total is None else total + spread
        total = join_rows(total, 6 * ZC)
        for side in range(2):
            for c in range(3):
                src[2 * j + side, c] = total[(3 * side + c) * ZC : (3 * side + c + 1) * ZC]


def march_kernel(line_bits, bits, chunks, wells_ref, near, far, out_ref, grid, field, src):
    share = 1 << (line_bits + bits)
    me = lax.axis_index("gx")
    sources(line_bits, bits, chunks, wells_ref, near, far, src)
    lane = lane_iota(ZC)
    own = lane < 64
    right = lane < 80
    even = on_even()
    left = lane >= 112

    for d in range(PLANES):
        for g in range(PAIRS):
            q, s = divmod(PAIRS * d + g, 4)
            x = chunks[d, g]
            after = jnp.where(even, near[q], far[q])
            before = jnp.where(even, far[q], near[q])
            for h in range(2):
                n = 2 * g + h
                if n == 27:
                    continue
                at = 16 * s + 64 * h
                edge = jnp.where(right, roll_lanes(after, 64 - at), roll_lanes(before, 112 - at))
                edge = jnp.where(jnp.logical_or(right, left), edge, 0.0)
                value = jnp.where(own, roll_lanes(x, 64 * h), edge)
                if n < 6:
                    value = value + src[d, n % 3]
                grid[d, n] = value

    state = None
    for i in range(PLANES):
        blocks = [grid[i, 6 + n] for n in range(9)]
        lower = [grid[i, 21 + c] for c in range(3)]
        upper = [grid[i, 24 + c] for c in range(3)]
        new = []
        for k in range(2):
            v = [grid[i, 3 * k + c] for c in range(3)]
            if i > 0:
                v = [v[c] - grid[i, 15 + c] * state[k][c] for c in range(3)]
            new.append(plane_apply(blocks, lower, upper, v))
        state = new
        for k in range(2):
            for c in range(3):
                field[i, 3 * k + c] = state[k][c]
    for i in range(PLANES - 2, -1, -1):
        blocks = [grid[i, 6 + n] for n in range(9)]
        lower = [grid[i, 21 + c] for c in range(3)]
        upper = [grid[i, 24 + c] for c in range(3)]
        new = []
        for k in range(2):
            v = [grid[i, 18 + c] * state[k][c] for c in range(3)]
            p = plane_apply(blocks, lower, upper, v)
            new.append([field[i, 3 * k + c] - p[c] for c in range(3)])
        state = new
        for k in range(2):
            for c in range(3):
                field[i, 3 * k + c] = state[k][c]

    for i in range(PLANES):
        for c in range(3):
            pair = jnp.where(own, field[i, c], roll_lanes(field[i, 3 + c], 64))
            out_ref[i, 2 * c] = pair[0:8]
            out_ref[i, 2 * c + 1] = pair[8:16]

    tiles = perf_tiles(chunks)
    parts = []
    for j in range(PLANES // 2):
        at_z, at_y = place_of(tiles[j], me * ZC)
        found = None
        for side, keep in enumerate(sides(at_z)):
            x = jnp.concatenate([field[2 * j + side, 3 + c] for c in range(3)], axis=0)
            got = join_rows(jnp.dot(split_rows(x), at_y, preferred_element_type=F32), 48)
            got = [jnp.where(keep, got[16 * c : 16 * c + 16], 0.0) for c in range(3)]
            found = got if found is None else [a + b for a, b in zip(found, got)]
        value = [jnp.sum(f, axis=0, keepdims=True) * tiles[j][2:3] for f in found]
        value = jnp.concatenate(value + [jnp.zeros((5, 128), F32)], axis=0)
        parts.append(jnp.concatenate(list(split3(value)) + [jnp.zeros((8, 128), F32)], axis=0).astype(BF16))
    wells = [ints(tile[1:2]) for tile in tiles]
    row = row_iota(128)
    for i in range(PLANES):
        total = jnp.zeros((32, 128), F32)
        for j in range(PLANES // 2):
            hot = jnp.where(wells[j] == row + share * i, 1.0, 0.0).astype(BF16)
            total += lax.dot_general(parts[j], hot, (((1,), (1,)), ((), ())), preferred_element_type=F32)
        out_ref[i, 6] = join_rows(total, 8)


def unpack_kernel(chunks, sums, out, wells, turned):
    held = wells.shape[1]
    total = sums[0]
    for b in range(1, sums.shape[0]):
        total = total + sums[b]
    shift = (128 - held * lax.axis_index("gy")) & 127
    wells[...] = pltpu.roll(total, shift, 1)[0:3, 0:held]
    for t in range(PLANES):
        for c in range(3):
            for h in range(2):
                turned[c, ZC * t + 8 * h : ZC * t + 8 * h + 8] = chunks[t, 2 * c + h]
    for c in range(3):
        y = turned[c].T
        out[0, c] = y[0:LINES]
        out[1, c] = y[LINES : 2 * LINES]


def call(kernel, inputs, out_shape, scratch=(), space=VMEM):
    if space is not VMEM:
        inputs = [pltpu.with_memory_space_constraint(x, space) for x in inputs]
        space = pl.BlockSpec(memory_space=space)
    return pl.pallas_call(
        kernel,
        out_shape=out_shape,
        in_specs=[space] * len(inputs),
        out_specs=jax.tree.map(lambda _: VMEM, out_shape),
        scratch_shapes=list(scratch),
        compiler_params=pltpu.CompilerParams(vmem_limit_bytes=VMEM_LIMIT),
    )(*inputs)


def shape(*dims):
    return jax.ShapeDtypeStruct(dims, F32)


def per_device(
    adjoint_rhs, block_inverse, x_couplings, y_couplings, perf_cell, perf_well, perf_weight, well_adjoint
):
    held = well_adjoint.shape[1]
    lines = lax.axis_size("gy")
    perfs = perf_cell.shape[0]

    packed = call(
        pack_kernel,
        [
            adjoint_rhs.reshape(6, LINES, 128),
            block_inverse.reshape(9, LINES, 128),
            x_couplings.reshape(6, LINES, 128),
            y_couplings.reshape(6, LINES, 128),
            perf_cell.reshape(1, perfs),
            perf_well.reshape(1, perfs),
            perf_weight.reshape(1, perfs),
            well_adjoint,
        ],
        shape(PLANES, PAIRS, ZC, 128),
        [
            pltpu.VMEM((6, LINES, 128), F32),
            pltpu.VMEM((9, LINES, 128), F32),
            pltpu.VMEM((6, LINES, 128), F32),
            pltpu.VMEM((6, LINES, 128), F32),
            pltpu.VMEM((1, perfs), jnp.int32),
            pltpu.VMEM((1, perfs), jnp.int32),
            pltpu.VMEM((1, perfs), F32),
            pltpu.VMEM((3, held), F32),
            pltpu.VMEM((ZC, 128), F32),
            pltpu.VMEM((PAIRS, 128, 128), F32),
            pltpu.SemaphoreType.DMA((8,)),
        ],
        space=pltpu.HBM,
    )
    chunks = lax.all_to_all(packed, "gx", 0, 0)

    strip = shape(STRIPS + 2, ZC, 128)
    near, far, wells = call(strip_kernel, [chunks], [strip, strip, shape(lines, PLANES, 128)])
    near = lax.ppermute(near, "gy", [(b, b ^ 1) for b in range(lines)])
    far = lax.ppermute(far, "gy", [(b, ((b + 1) ^ 1) - 1) for b in range(1, lines - 1)])

    wells = lax.all_to_all(wells, "gy", 0, 0)

    back = call(
        functools.partial(march_kernel, lines.bit_length() - 1, held.bit_length() - 1),
        [chunks, wells, near, far],
        shape(PLANES, 7, 8, 128),
        [
            pltpu.VMEM((PLANES, 27, ZC, 128), F32),
            pltpu.VMEM((PLANES, 6, ZC, 128), F32),
            pltpu.VMEM((PLANES, 3, ZC, 128), F32),
        ],
    )
    got = lax.all_to_all(back, "gx", 0, 0)
    sums = jnp.broadcast_to(jnp.sum(got[:, 6], axis=0), (lines, 8, 128))
    sums = lax.all_to_all(sums, "gy", 0, 0)
    precond, well_update = call(
        unpack_kernel,
        [got, sums],
        [shape(2, 3, LINES, 128), shape(3, held)],
        [pltpu.VMEM((3, 128, 128), F32)],
    )
    return precond.reshape(adjoint_rhs.shape), well_update


def solution(mesh):
    placed = (
        P(None, None, "gx", "gy", None),
        P(None, None, "gx", "gy", None),
        P(None, None, "gx", "gy", None),
        P(None, None, "gx", "gy", None),
        P(("gx", "gy")),
        P(("gx", "gy")),
        P(("gx", "gy")),
        P(None, ("gx", "gy")),
    )
    return jax.shard_map(
        per_device,
        mesh=mesh,
        in_specs=placed,
        out_specs=(P(None, None, "gx", "gy", None), P(None, ("gx", "gy"))),
        check_vma=False,
    )
```

time: 95.3 us -> 85.8 us (0.900)
  waiting for transfers between devices: 5.41 us -> 0.01 us
  blocking collectives: 74.4 us -> 73.2 us
  starting transfers between devices: 6.36 us -> 5.21 us
  Pallas kernels: 7.47 us -> 6.42 us
    ppermute x2, waiting for transfers between devices: 5.41 us -> 0.01 us  [the longest x1 0.01 us: per_device(): lax.ppermute(far, 'gy', [(b, (b + 1 ^ 1) - 1) for b in range(1, lines - 1)])]
    all_to_all x1, blocking collectives: 15.1 us -> 11.3 us  [per_device(): sums = lax.all_to_all(sums, 'gy', 0, 0)]
    all_to_all x1, blocking collectives: 11.4 us -> 13.9 us  [per_device(): got = lax.all_to_all(back, 'gx', 0, 0)]
    ppermute x2, starting transfers between devices: 6.36 us -> 5.21 us  [the longest x1 3.02 us: per_device(): lax.ppermute(far, 'gy', [(b, (b + 1 ^ 1) - 1) for b in range(1, lines - 1)])]
    pallas_call x6 -> x4, Pallas kernels: 7.47 us -> 6.42 us  [call(): pl.pallas_call(kernel, out_shape=out_shape, in_specs=[space] * len(inputs...]
    all_to_all x1, blocking collectives: 15.3 us -> 14.3 us  [per_device(): wells = lax.all_to_all(wells, 'gy', 0, 0)]
  transfers between devices with their start and end apart: 2 -> 2, of which waited for: 2 -> 0; matrix products, arithmetic and copies ran while one was open for 0% -> 0% of each run, Pallas kernels for 0% -> 0%
where the time goes in v3:
time: 85.8 us; the launch traced here: 85.5 us
  blocking collectives  73.2 us (85%)
  Pallas kernels  6.42 us (7%)
  starting transfers between devices  5.21 us (6%)
    all_to_all x1, blocking collectives, per_device(): chunks = lax.all_to_all(packed, 'gx', 0, 0)  33.6 us
    all_to_all x1, blocking collectives, per_device(): wells = lax.all_to_all(wells, 'gy', 0, 0)  14.3 us
    all_to_all x1, blocking collectives, per_device(): got = lax.all_to_all(back, 'gx', 0, 0)  13.9 us
    all_to_all x1, blocking collectives, per_device(): sums = lax.all_to_all(sums, 'gy', 0, 0)  11.3 us
    pallas_call x4, Pallas kernels, call(): pl.pallas_call(kernel, out_shape=out_shape, in_specs=[space] * len(inputs...  6.42 us
    ppermute x1, starting transfers between devices, per_device(): lax.ppermute(far, 'gy', [(b, (b + 1 ^ 1) - 1) for b in range(1, lines - 1)])  3.02 us
    ppermute x1, starting transfers between devices, per_device(): near = lax.ppermute(near, 'gy', [(b, b ^ 1) for b in range(lines)])  2.19 us
  transfers between devices with their start and end apart: 2, of which 0 were waited for; matrix products, arithmetic and copies ran while one was open for 0% of the time, Pallas kernels for 0%

profile of v3, /device:TPU:1, one launch (start us, length us, event | category | flops | bytes accessed | tf_op | source)
XLA Modules:
  0.0 85.5 jit_solution(4399333210297103637)
XLA Ops:
  0.6 1.8 %shard_map.95 = f32[8,14,16,128]{3,2,1,0:T(8,128)S(1)} custom-call(f32[6,64,128]{2,1,0:T(8,128)} %bitcast.11, f32[9,64,128]{2,1,0:T(8,128)} %bitcast.10, f32[6,64,128]{2,1,0:T(8,128)} %bitcast.12, f32[6,64,128]{2,1,0:T(8,128)} %bitcast.13, s32[1,64]{1,0:T(1,128)} %bitcast.14, s32[1,64]{1,0:T(1,128)} %bitcast.15, f32[1,64]{1,0:T(1,128)} %bitcast.16, f32[3,4]{1,0:T(4,128)} %wells.1), custom_call_target="tpu_custom_call" | custom-call | tf_op jit(solution)/shard_map/pallas_call | solution.py:319
  2.4 33.6 %all_to_all.20.chunks = f32[8,14,16,128]{3,2,1,0:T(8,128)S(1)} all-to-all(f32[8,14,16,128]{3,2,1,0:T(8,128)S(1)} %shard_map.95), channel_id=1, replica_groups=mesh['gx'=8,'gy'=32] {'gx'}, dimensions={0} | all-to-all | bytes 1835008 | tf_op jit(solution)/shard_map/all_to_all | solution.py:368
  36.0 0.4 shard_map.96
  36.4 2.2 %collective-permute-start = (f32[30,16,128]{2,1,0:T(8,128)S(1)}, f32[30,16,128]{2,1,0:T(8,128)S(1)}, u32[]{:S(2)}, u32[]{:S(2)}) collective-permute-start(f32[30,16,128]{2,1,0:T(8,128)S(1)} %get-tuple-element.8), channel_id=1, source_target_pairs={{0,1},{1,0},{2,3},{3,2},{4,5},{5,4},{6,7},{7,6},{8,9},{9,8},{10,11... | collective-permute-start | bytes 737288 | tf_op jit(solution)/shard_map/ppermute | solution.py:372
  38.6 3.0 %collective-permute-start.1 = (f32[30,16,128]{2,1,0:T(8,128)S(1)}, f32[30,16,128]{2,1,0:T(8,128)S(1)}, u32[]{:S(2)}, u32[]{:S(2)}) collective-permute-start(f32[30,16,128]{2,1,0:T(8,128)S(1)} %get-tuple-element.9), channel_id=1, source_target_pairs={{1,2},{2,1},{3,4},{4,3},{5,6},{6,5},{7,8},{8,7},{9,10},{10,9},{11,... | collective-permute-start | bytes 737288 | tf_op jit(solution)/shard_map/ppermute | solution.py:373
  41.6 14.3 %all_to_all.21.wells_ref = f32[32,8,128]{2,1,0:T(8,128)S(1)} all-to-all(f32[32,8,128]{2,1,0:T(8,128)S(1)} %get-tuple-element.7), channel_id=1, replica_groups=mesh['gx'=8,'gy'=32] {'gy'}, dimensions={0} | all-to-all | bytes 262144 | tf_op jit(solution)/shard_map/all_to_all | solution.py:375
  56.0 0.0 collective-permute-done.near
  56.0 0.0 collective-permute-done.1.far
  56.0 3.4 %shard_map.97 = f32[8,7,8,128]{3,2,1,0:T(8,128)S(1)} custom-call(f32[8,14,16,128]{3,2,1,0:T(8,128)S(1)} %all_to_all.20.chunks, f32[32,8,128]{2,1,0:T(8,128)S(1)} %all_to_all.21.wells_ref, f32[30,16,128]{2,1,0:T(8,128)S(1)} %collective-permute-done.near, f32[30,16,128]{2,1,0:T(8,128)S(1)} %collective-permute-done.1.far), custom_call_target="tpu_custom_call" | custom-call | tf_op jit(solution)/shard_map/pallas_call | solution.py:319
  59.4 13.9 %all_to_all.22.chunks = f32[8,7,8,128]{3,2,1,0:T(8,128)S(1)} all-to-all(f32[8,7,8,128]{3,2,1,0:T(8,128)S(1)} %shard_map.97), channel_id=1, replica_groups=mesh['gx'=8,'gy'=32] {'gx'}, dimensions={0} | all-to-all | bytes 458752 | tf_op jit(solution)/shard_map/all_to_all | solution.py:387
  73.3 11.3 %all_to_all.23.sums = f32[32,8,128]{2,1,0:T(8,128)S(1)} all-to-all(f32[32,8,128]{2,1,0:T(8,128)S(1)} %broadcast_in_dim.3), channel_id=1, replica_groups=mesh['gx'=8,'gy'=32] {'gy'}, dimensions={0} | all-to-all | bytes 262144 | tf_op jit(solution)/shard_map/all_to_all | solution.py:389
  84.7 0.8 shard_map.98
  (2 shorter events, 0.0 us)
Async XLA Ops:
  36.4 19.6 %collective-permute-start = (f32[30,16,128]{2,1,0:T(8,128)S(1)}, f32[30,16,128]{2,1,0:T(8,128)S(1)}, u32[]{:S(2)}, u32[]{:S(2)}) collective-permute-start(f32[30,16,128]{2,1,0:T(8,128)S(1)} %get-tuple-element.8), channel_id=1, source_target_pairs={{0,1},{1,0},{2,3},{3,2},{4,5},{5,4},{6,7},{7,6},{8,9},{9,8},{10,11... | collective-permute-start | bytes 737288 | tf_op jit(solution)/shard_map/ppermute | solution.py:372
  38.6 17.4 %collective-permute-start.1 = (f32[30,16,128]{2,1,0:T(8,128)S(1)}, f32[30,16,128]{2,1,0:T(8,128)S(1)}, u32[]{:S(2)}, u32[]{:S(2)}) collective-permute-start(f32[30,16,128]{2,1,0:T(8,128)S(1)} %get-tuple-element.9), channel_id=1, source_target_pairs={{1,2},{2,1},{3,4},{4,3},{5,6},{6,5},{7,8},{8,7},{9,10},{10,9},{11,... | collective-permute-start | bytes 737288 | tf_op jit(solution)/shard_map/ppermute | solution.py:373

commit v4 on v3

--- a/solution.py
+++ b/solution.py
@@ -13,7 +13,6 @@
 LINES = 64
 ZC = 16
 PAIRS = 14
-STRIP = 16
 WELL_ROW = 3
 STRIPS = PLANES * PAIRS // 4
 VMEM_LIMIT = 24 * 1024 * 1024
@@ -128,10 +127,6 @@
     return at_z, at_y
 
 
-def on_even():
-    return jnp.zeros((ZC, 128), jnp.int32) + (lax.axis_index("gy") & 1) == 0
-
-
 def sides(at_z):
     low = lane_iota(ZC) < 64
     return [jnp.logical_and(at_z, low), jnp.logical_and(at_z, jnp.logical_not(low))]
@@ -146,19 +141,19 @@
         pair = jnp.concatenate([tiles[2 * u], tiles[2 * u + 1]], axis=0)
         near_ref[STRIPS + u] = pair
         far_ref[STRIPS + u] = pair
-    slot = (lane_iota(ZC) & 63) >> 4
-    even = on_even()
-    for q in range(PLANES * PAIRS // 4):
-        first = last = None
+    lane = lane_iota(ZC)
+    odd = lax.axis_index("gy") & 1
+    near_slot = ((lane - 48 * (1 - odd)) & 63) >> 4
+    far_slot = ((lane - 48 * odd) & 63) >> 4
+    for q in range(STRIPS):
+        near = far = None
         for s in range(4):
             d, g = divmod(4 * q + s, PAIRS)
-            x = chunks[d, g]
-            a = roll_lanes(x, 16 * s)
-            b = roll_lanes(x, 16 * s + 80)
-            first = a if s == 0 else jnp.where(slot == s, a, first)
-            last = b if s == 0 else jnp.where(slot == s, b, last)
-        near_ref[q] = jnp.where(even, last, first)
-        far_ref[q] = jnp.where(even, first, last)
+            x = roll_lanes(chunks[d, g], 16 * s)
+            near = x if s == 0 else jnp.where(near_slot == s, x, near)
+            far = x if s == 0 else jnp.where(far_slot == s, x, far)
+        near_ref[q] = near
+        far_ref[q] = far
 
 
 def block_apply(blocks, v):
@@ -210,32 +205,50 @@
 
 
 def march_kernel(line_bits, bits, chunks, wells_ref, near, far, out_ref, grid, field, src):
-    share = 1 << (line_bits + bits)
+    share = line_bits + bits
     me = lax.axis_index("gx")
     sources(line_bits, bits, chunks, wells_ref, near, far, src)
     lane = lane_iota(ZC)
     own = lane < 64
-    right = lane < 80
-    even = on_even()
-    left = lane >= 112
+    odd = lax.axis_index("gy") & 1
+    slot = lane >> 4
+    outside = jnp.logical_or(lane < 80, lane >= 112)
 
     for d in range(PLANES):
         for g in range(PAIRS):
             q, s = divmod(PAIRS * d + g, 4)
             x = chunks[d, g]
-            after = jnp.where(even, near[q], far[q])
-            before = jnp.where(even, far[q], near[q])
+            ends = (near[q], far[q])
             for h in range(2):
                 n = 2 * g + h
                 if n == 27:
                     continue
                 at = 16 * s + 64 * h
-                edge = jnp.where(right, roll_lanes(after, 64 - at), roll_lanes(before, 112 - at))
-                edge = jnp.where(jnp.logical_or(right, left), edge, 0.0)
+                first = at // 16
+                edge = jnp.where(slot == ((first + 3 * odd) & 7), *ends)
+                edge = jnp.where(outside, roll_lanes(edge, 64 - at), 0.0)
                 value = jnp.where(own, roll_lanes(x, 64 * h), edge)
                 if n < 6:
                     value = value + src[d, n % 3]
                 grid[d, n] = value
+
+    tiles = perf_tiles(chunks)
+    row = row_iota(128)
+    places = [place_of(tile, me * ZC) for tile in tiles]
+    found = [None] * (PLANES // 2)
+
+    def finish(i, planes):
+        for c in range(3):
+            pair = jnp.where(own, planes[0][c], roll_lanes(planes[1][c], 64))
+            out_ref[i, 2 * c] = pair[0:8]
+            out_ref[i, 2 * c + 1] = pair[8:16]
+        at_z, at_y = places[i // 2]
+        x = split_rows(jnp.concatenate(planes[1], axis=0))
+        got = join_rows(jnp.dot(x, at_y, preferred_element_type=F32), 48)
+        keep = sides(at_z)[i % 2]
+        got = [jnp.where(keep, got[16 * c : 16 * c + 16], 0.0) for c in range(3)]
+        sofar = found[i // 2]
+        found[i // 2] = got if sofar is None else [a + b for a, b in zip(sofar, got)]
 
     state = None
     for i in range(PLANES):
@@ -249,9 +262,11 @@
                 v = [v[c] - grid[i, 15 + c] * state[k][c] for c in range(3)]
             new.append(plane_apply(blocks, lower, upper, v))
         state = new
-        for k in range(2):
-            for c in range(3):
-                field[i, 3 * k + c] = state[k][c]
+        if i < PLANES - 1:
+            for k in range(2):
+                for c in range(3):
+                    field[i, 3 * k + c] = state[k][c]
+    finish(PLANES - 1, state)
     for i in range(PLANES - 2, -1, -1):
         blocks = [grid[i, 6 + n] for n in range(9)]
         lower = [grid[i, 21 + c] for c in range(3)]
@@ -262,37 +277,20 @@
             p = plane_apply(blocks, lower, upper, v)
             new.append([field[i, 3 * k + c] - p[c] for c in range(3)])
         state = new
-        for k in range(2):
-            for c in range(3):
-                field[i, 3 * k + c] = state[k][c]
-
+        finish(i, state)
+
+    total = None
+    for j in range(PLANES // 2):
+        well = ints(tiles[j][1:2])
+        value = [jnp.sum(f, axis=0, keepdims=True) * tiles[j][2:3] for f in found[j]]
+        rows = [jnp.where((well >> share) == i, v, 0.0) for i in range(PLANES) for v in value]
+        rows = jnp.concatenate(list(split3(jnp.concatenate(rows, axis=0))) + [jnp.zeros((8, 128), F32)], axis=0)
+        hot = jnp.where((well & ((1 << share) - 1)) == row, 1.0, 0.0).astype(BF16)
+        part = lax.dot_general(rows.astype(BF16), hot, (((1,), (1,)), ((), ())), preferred_element_type=F32)
+        total = part if total is None else total + part
+    total = join_rows(total, 3 * PLANES)
     for i in range(PLANES):
-        for c in range(3):
-            pair = jnp.where(own, field[i, c], roll_lanes(field[i, 3 + c], 64))
-            out_ref[i, 2 * c] = pair[0:8]
-            out_ref[i, 2 * c + 1] = pair[8:16]
-
-    tiles = perf_tiles(chunks)
-    parts = []
-    for j in range(PLANES // 2):
-        at_z, at_y = place_of(tiles[j], me * ZC)
-        found = None
-        for side, keep in enumerate(sides(at_z)):
-            x = jnp.concatenate([field[2 * j + side, 3 + c] for c in range(3)], axis=0)
-            got = join_rows(jnp.dot(split_rows(x), at_y, preferred_element_type=F32), 48)
-            got = [jnp.where(keep, got[16 * c : 16 * c + 16], 0.0) for c in range(3)]
-            found = got if found is None else [a + b for a, b in zip(found, got)]
-        value = [jnp.sum(f, axis=0, keepdims=True) * tiles[j][2:3] for f in found]
-        value = jnp.concatenate(value + [jnp.zeros((5, 128), F32)], axis=0)
-        parts.append(jnp.concatenate(list(split3(value)) + [jnp.zeros((8, 128), F32)], axis=0).astype(BF16))
-    wells = [ints(tile[1:2]) for tile in tiles]
-    row = row_iota(128)
-    for i in range(PLANES):
-        total = jnp.zeros((32, 128), F32)
-        for j in range(PLANES // 2):
-            hot = jnp.where(wells[j] == row + share * i, 1.0, 0.0).astype(BF16)
-            total += lax.dot_general(parts[j], hot, (((1,), (1,)), ((), ())), preferred_element_type=F32)
-        out_ref[i, 6] = join_rows(total, 8)
+        out_ref[i, 6] = jnp.concatenate([total[3 * i : 3 * i + 3], jnp.zeros((5, 128), F32)], axis=0)
 
 
 def unpack_kernel(chunks, sums, out, wells, turned):

time: 85.8 us -> 84.8 us (0.988)
  Pallas kernels: 6.42 us -> 5.45 us
    pallas_call x4, Pallas kernels: 6.42 us -> 5.45 us  [call(): pl.pallas_call(kernel, out_shape=out_shape, in_specs=[space] * len(inputs...]
where the time goes in v4:
time: 84.8 us; the launch traced here: 84.5 us
  blocking collectives  73.2 us (86%)
  Pallas kernels  5.45 us (6%)
  starting transfers between devices  5.21 us (6%)
    all_to_all x1, blocking collectives, per_device(): chunks = lax.all_to_all(packed, 'gx', 0, 0)  33.6 us
    all_to_all x1, blocking collectives, per_device(): wells = lax.all_to_all(wells, 'gy', 0, 0)  14.3 us
    all_to_all x1, blocking collectives, per_device(): got = lax.all_to_all(back, 'gx', 0, 0)  13.9 us
    all_to_all x1, blocking collectives, per_device(): sums = lax.all_to_all(sums, 'gy', 0, 0)  11.3 us
    pallas_call x4, Pallas kernels, call(): pl.pallas_call(kernel, out_shape=out_shape, in_specs=[space] * len(inputs...  5.45 us
    ppermute x1, starting transfers between devices, per_device(): lax.ppermute(far, 'gy', [(b, (b + 1 ^ 1) - 1) for b in range(1, lines - 1)])  3.02 us
    ppermute x1, starting transfers between devices, per_device(): near = lax.ppermute(near, 'gy', [(b, b ^ 1) for b in range(lines)])  2.19 us
  transfers between devices with their start and end apart: 2, of which 0 were waited for; matrix products, arithmetic and copies ran while one was open for 0% of the time, Pallas kernels for 0%

profile of v4, /device:TPU:1, one launch (start us, length us, event | category | flops | bytes accessed | tf_op | source)
XLA Modules:
  0.0 84.5 jit_solution(17438013722590115343)
XLA Ops:
  0.6 1.8 %shard_map.95 = f32[8,14,16,128]{3,2,1,0:T(8,128)S(1)} custom-call(f32[6,64,128]{2,1,0:T(8,128)} %bitcast.11, f32[9,64,128]{2,1,0:T(8,128)} %bitcast.10, f32[6,64,128]{2,1,0:T(8,128)} %bitcast.12, f32[6,64,128]{2,1,0:T(8,128)} %bitcast.13, s32[1,64]{1,0:T(1,128)} %bitcast.14, s32[1,64]{1,0:T(1,128)} %bitcast.15, f32[1,64]{1,0:T(1,128)} %bitcast.16, f32[3,4]{1,0:T(4,128)} %wells.1), custom_call_target="tpu_custom_call" | custom-call | tf_op jit(solution)/shard_map/pallas_call | solution.py:317
  2.4 33.6 %all_to_all.20.chunks = f32[8,14,16,128]{3,2,1,0:T(8,128)S(1)} all-to-all(f32[8,14,16,128]{3,2,1,0:T(8,128)S(1)} %shard_map.95), channel_id=1, replica_groups=mesh['gx'=8,'gy'=32] {'gx'}, dimensions={0} | all-to-all | bytes 1835008 | tf_op jit(solution)/shard_map/all_to_all | solution.py:366
  36.0 0.2 shard_map.96
  36.2 2.2 %collective-permute-start = (f32[30,16,128]{2,1,0:T(8,128)S(1)}, f32[30,16,128]{2,1,0:T(8,128)S(1)}, u32[]{:S(2)}, u32[]{:S(2)}) collective-permute-start(f32[30,16,128]{2,1,0:T(8,128)S(1)} %get-tuple-element.8), channel_id=1, source_target_pairs={{0,1},{1,0},{2,3},{3,2},{4,5},{5,4},{6,7},{7,6},{8,9},{9,8},{10,11... | collective-permute-start | bytes 737288 | tf_op jit(solution)/shard_map/ppermute | solution.py:370
  38.4 3.0 %collective-permute-start.1 = (f32[30,16,128]{2,1,0:T(8,128)S(1)}, f32[30,16,128]{2,1,0:T(8,128)S(1)}, u32[]{:S(2)}, u32[]{:S(2)}) collective-permute-start(f32[30,16,128]{2,1,0:T(8,128)S(1)} %get-tuple-element.9), channel_id=1, source_target_pairs={{1,2},{2,1},{3,4},{4,3},{5,6},{6,5},{7,8},{8,7},{9,10},{10,9},{11,... | collective-permute-start | bytes 737288 | tf_op jit(solution)/shard_map/ppermute | solution.py:371
  41.5 14.3 %all_to_all.21.wells_ref = f32[32,8,128]{2,1,0:T(8,128)S(1)} all-to-all(f32[32,8,128]{2,1,0:T(8,128)S(1)} %get-tuple-element.7), channel_id=1, replica_groups=mesh['gx'=8,'gy'=32] {'gy'}, dimensions={0} | all-to-all | bytes 262144 | tf_op jit(solution)/shard_map/all_to_all | solution.py:373
  55.8 0.0 collective-permute-done.near
  55.8 0.0 collective-permute-done.1.far
  55.8 2.6 %shard_map.97 = f32[8,7,8,128]{3,2,1,0:T(8,128)S(1)} custom-call(f32[8,14,16,128]{3,2,1,0:T(8,128)S(1)} %all_to_all.20.chunks, f32[32,8,128]{2,1,0:T(8,128)S(1)} %all_to_all.21.wells_ref, f32[30,16,128]{2,1,0:T(8,128)S(1)} %collective-permute-done.near, f32[30,16,128]{2,1,0:T(8,128)S(1)} %collective-permute-done.1.far), custom_call_target="tpu_custom_call" | custom-call | tf_op jit(solution)/shard_map/pallas_call | solution.py:317
  58.4 13.9 %all_to_all.22.chunks = f32[8,7,8,128]{3,2,1,0:T(8,128)S(1)} all-to-all(f32[8,7,8,128]{3,2,1,0:T(8,128)S(1)} %shard_map.97), channel_id=1, replica_groups=mesh['gx'=8,'gy'=32] {'gx'}, dimensions={0} | all-to-all | bytes 458752 | tf_op jit(solution)/shard_map/all_to_all | solution.py:385
  72.4 11.3 %all_to_all.23.sums = f32[32,8,128]{2,1,0:T(8,128)S(1)} all-to-all(f32[32,8,128]{2,1,0:T(8,128)S(1)} %broadcast_in_dim.3), channel_id=1, replica_groups=mesh['gx'=8,'gy'=32] {'gy'}, dimensions={0} | all-to-all | bytes 262144 | tf_op jit(solution)/shard_map/all_to_all | solution.py:387
  83.7 0.8 shard_map.98
  (2 shorter events, 0.0 us)
Async XLA Ops:
  36.2 19.6 %collective-permute-start = (f32[30,16,128]{2,1,0:T(8,128)S(1)}, f32[30,16,128]{2,1,0:T(8,128)S(1)}, u32[]{:S(2)}, u32[]{:S(2)}) collective-permute-start(f32[30,16,128]{2,1,0:T(8,128)S(1)} %get-tuple-element.8), channel_id=1, source_target_pairs={{0,1},{1,0},{2,3},{3,2},{4,5},{5,4},{6,7},{7,6},{8,9},{9,8},{10,11... | collective-permute-start | bytes 737288 | tf_op jit(solution)/shard_map/ppermute | solution.py:370
  38.4 17.4 %collective-permute-start.1 = (f32[30,16,128]{2,1,0:T(8,128)S(1)}, f32[30,16,128]{2,1,0:T(8,128)S(1)}, u32[]{:S(2)}, u32[]{:S(2)}) collective-permute-start(f32[30,16,128]{2,1,0:T(8,128)S(1)} %get-tuple-element.9), channel_id=1, source_target_pairs={{1,2},{2,1},{3,4},{4,3},{5,6},{6,5},{7,8},{8,7},{9,10},{10,9},{11,... | collective-permute-start | bytes 737288 | tf_op jit(solution)/shard_map/ppermute | solution.py:371

commit v5 on v4

--- a/solution.py
+++ b/solution.py
@@ -133,9 +133,12 @@
 
 
 def strip_kernel(chunks, near_ref, far_ref, wells_ref):
-    last = PAIRS - 1
-    own = jnp.concatenate([chunks[d, last, WELL_ROW : WELL_ROW + 1] for d in range(PLANES)], axis=0)
-    wells_ref[...] = jnp.broadcast_to(roll_lanes(own, 64)[None], wells_ref.shape)
+    own = jnp.zeros((1, 128), F32)
+    held_lanes = (lane_iota(1) >> 4) == 4
+    for d in range(PLANES):
+        row = jnp.where(held_lanes, chunks[d, PAIRS - 1, WELL_ROW : WELL_ROW + 1], 0.0)
+        own = own + roll_lanes(row, 64 + ZC * d)
+    wells_ref[...] = jnp.broadcast_to(own, wells_ref.shape)
     tiles = perf_tiles(chunks)
     for u in range(2):
         pair = jnp.concatenate([tiles[2 * u], tiles[2 * u + 1]], axis=0)
@@ -169,7 +172,18 @@
 def sources(line_bits, bits, chunks, wells_ref, near, far, src):
     held = 1 << bits
     first_z = lax.axis_index("gx") * ZC
-    wells = split_rows(wells_ref[...].reshape(-1, 128).T[0:ZC])
+    rows = wells_ref[...]
+    turned = jnp.concatenate([rows, jnp.zeros((128 - rows.shape[0], 128), F32)], axis=0).T
+    quarter = lane_iota(ZC) >> 5
+    wells = []
+    for u in range(2):
+        tile = None
+        for v in range(4):
+            d = 4 * u + v
+            part = roll_lanes(turned[ZC * d : ZC * d + ZC], 32 * v)
+            tile = part if v == 0 else jnp.where(quarter == v, part, tile)
+        wells.append(tile)
+    wells = split_rows(jnp.concatenate(wells, axis=1))
     own = perf_tiles(chunks)
     row = row_iota(128)
     odd = lax.axis_index("gy") & 1
@@ -181,7 +195,7 @@
         for tile, span, base in zip([own[j], near[STRIPS + j // 2, half], far[STRIPS + j // 2, half]], spans, (0, 64, 64)):
             well = ints(tile[1:2])
             owner = well >> bits
-            at = (owner & ((1 << line_bits) - 1)) * PLANES + (owner >> line_bits)
+            at = (owner >> line_bits) * 32 + (owner & ((1 << line_bits) - 1))
             hot = jnp.where(at == row_iota(wells.shape[1]), 1.0, 0.0).astype(BF16)
             picked = join_rows(jnp.dot(wells, hot, preferred_element_type=F32), ZC)
             terms = []
@@ -366,11 +380,11 @@
     chunks = lax.all_to_all(packed, "gx", 0, 0)
 
     strip = shape(STRIPS + 2, ZC, 128)
-    near, far, wells = call(strip_kernel, [chunks], [strip, strip, shape(lines, PLANES, 128)])
+    near, far, wells = call(strip_kernel, [chunks], [strip, strip, shape(lines, 128)])
     near = lax.ppermute(near, "gy", [(b, b ^ 1) for b in range(lines)])
     far = lax.ppermute(far, "gy", [(b, ((b + 1) ^ 1) - 1) for b in range(1, lines - 1)])
 
-    wells = lax.all_to_all(wells, "gy", 0, 0)
+    wells = lax.all_to_all(wells, "gy", 0, 0, tiled=True)
 
     back = call(
         functools.partial(march_kernel, lines.bit_length() - 1, held.bit_length() - 1),

time: 84.8 us -> 84.2 us (level)
    all_to_all x1, blocking collectives: 13.9 us -> 12.6 us  [per_device(): got = lax.all_to_all(back, 'gx', 0, 0)]
    all_to_all x1, blocking collectives: 11.3 us -> 12.6 us  [per_device(): sums = lax.all_to_all(sums, 'gy', 0, 0)]
where the time goes in v5:
time: 84.2 us; the launch traced here: 83.9 us
  blocking collectives  72.4 us (86%)
  Pallas kernels  5.54 us (7%)
  starting transfers between devices  5.21 us (6%)
    all_to_all x1, blocking collectives, per_device(): chunks = lax.all_to_all(packed, 'gx', 0, 0)  33.6 us
    all_to_all x1, blocking collectives, per_device(): wells = lax.all_to_all(wells, 'gy', 0, 0, tiled=True)  13.6 us
    all_to_all x1, blocking collectives, per_device(): sums = lax.all_to_all(sums, 'gy', 0, 0)  12.6 us
    all_to_all x1, blocking collectives, per_device(): got = lax.all_to_all(back, 'gx', 0, 0)  12.6 us
    pallas_call x4, Pallas kernels, call(): pl.pallas_call(kernel, out_shape=out_shape, in_specs=[space] * len(inputs...  5.54 us
    ppermute x1, starting transfers between devices, per_device(): lax.ppermute(far, 'gy', [(b, (b + 1 ^ 1) - 1) for b in range(1, lines - 1)])  3.02 us
    ppermute x1, starting transfers between devices, per_device(): near = lax.ppermute(near, 'gy', [(b, b ^ 1) for b in range(lines)])  2.19 us
  transfers between devices with their start and end apart: 2, of which 0 were waited for; matrix products, arithmetic and copies ran while one was open for 0% of the time, Pallas kernels for 0%

profile of v5, /device:TPU:1, one launch (start us, length us, event | category | flops | bytes accessed | tf_op | source)
XLA Modules:
  0.0 83.9 jit_solution(17498798286594133970)
XLA Ops:
  0.6 1.8 %shard_map.95 = f32[8,14,16,128]{3,2,1,0:T(8,128)S(1)} custom-call(f32[6,64,128]{2,1,0:T(8,128)} %bitcast.17, f32[9,64,128]{2,1,0:T(8,128)} %bitcast.16, f32[6,64,128]{2,1,0:T(8,128)} %bitcast.18, f32[6,64,128]{2,1,0:T(8,128)} %bitcast.19, s32[1,64]{1,0:T(1,128)} %bitcast.20, s32[1,64]{1,0:T(1,128)} %bitcast.21, f32[1,64]{1,0:T(1,128)} %bitcast.22, f32[3,4]{1,0:T(4,128)} %wells.1), custom_call_target="tpu_custom_call" | custom-call | tf_op jit(solution)/shard_map/pallas_call | solution.py:331
  2.4 33.6 %all_to_all.26.chunks = f32[8,14,16,128]{3,2,1,0:T(8,128)S(1)} all-to-all(f32[8,14,16,128]{3,2,1,0:T(8,128)S(1)} %shard_map.95), channel_id=1, replica_groups=mesh['gx'=8,'gy'=32] {'gx'}, dimensions={0} | all-to-all | bytes 1835008 | tf_op jit(solution)/shard_map/all_to_all | solution.py:380
  36.0 0.3 shard_map.96
  36.2 2.2 %collective-permute-start = (f32[30,16,128]{2,1,0:T(8,128)S(1)}, f32[30,16,128]{2,1,0:T(8,128)S(1)}, u32[]{:S(2)}, u32[]{:S(2)}) collective-permute-start(f32[30,16,128]{2,1,0:T(8,128)S(1)} %get-tuple-element.8), channel_id=1, source_target_pairs={{0,1},{1,0},{2,3},{3,2},{4,5},{5,4},{6,7},{7,6},{8,9},{9,8},{10,11... | collective-permute-start | bytes 737288 | tf_op jit(solution)/shard_map/ppermute | solution.py:384
  38.4 3.0 %collective-permute-start.1 = (f32[30,16,128]{2,1,0:T(8,128)S(1)}, f32[30,16,128]{2,1,0:T(8,128)S(1)}, u32[]{:S(2)}, u32[]{:S(2)}) collective-permute-start(f32[30,16,128]{2,1,0:T(8,128)S(1)} %get-tuple-element.9), channel_id=1, source_target_pairs={{1,2},{2,1},{3,4},{4,3},{5,6},{6,5},{7,8},{8,7},{9,10},{10,9},{11,... | collective-permute-start | bytes 737288 | tf_op jit(solution)/shard_map/ppermute | solution.py:385
  41.5 13.6 %all_to_all.27 = f32[32,1,128]{2,1,0:T(1,128)S(1)} all-to-all(f32[32,1,128]{2,1,0:T(1,128)S(1)} %bitcast.15), channel_id=1, replica_groups=mesh['gx'=8,'gy'=32] {'gy'}, dimensions={0} | all-to-all | bytes 32768 | tf_op jit(solution)/shard_map/all_to_all | solution.py:387
  55.1 0.0 collective-permute-done.near
  55.1 0.0 collective-permute-done.1.far
  55.1 2.7 %shard_map.97 = f32[8,7,8,128]{3,2,1,0:T(8,128)S(1)} custom-call(f32[8,14,16,128]{3,2,1,0:T(8,128)S(1)} %all_to_all.26.chunks, f32[32,128]{1,0:T(8,128)S(1)} %bitcast.14, f32[30,16,128]{2,1,0:T(8,128)S(1)} %collective-permute-done.near, f32[30,16,128]{2,1,0:T(8,128)S(1)} %collective-permute-done.1.far), custom_call_target="tpu_custom_call" | custom-call | tf_op jit(solution)/shard_map/pallas_call | solution.py:331
  57.8 12.6 %all_to_all.28.chunks = f32[8,7,8,128]{3,2,1,0:T(8,128)S(1)} all-to-all(f32[8,7,8,128]{3,2,1,0:T(8,128)S(1)} %shard_map.97), channel_id=1, replica_groups=mesh['gx'=8,'gy'=32] {'gx'}, dimensions={0} | all-to-all | bytes 458752 | tf_op jit(solution)/shard_map/all_to_all | solution.py:399
  70.4 12.6 %all_to_all.29.sums = f32[32,8,128]{2,1,0:T(8,128)S(1)} all-to-all(f32[32,8,128]{2,1,0:T(8,128)S(1)} %broadcast_in_dim.3), channel_id=1, replica_groups=mesh['gx'=8,'gy'=32] {'gy'}, dimensions={0} | all-to-all | bytes 262144 | tf_op jit(solution)/shard_map/all_to_all | solution.py:401
  83.1 0.8 shard_map.98
  (2 shorter events, 0.0 us)
Async XLA Ops:
  36.2 18.9 %collective-permute-start = (f32[30,16,128]{2,1,0:T(8,128)S(1)}, f32[30,16,128]{2,1,0:T(8,128)S(1)}, u32[]{:S(2)}, u32[]{:S(2)}) collective-permute-start(f32[30,16,128]{2,1,0:T(8,128)S(1)} %get-tuple-element.8), channel_id=1, source_target_pairs={{0,1},{1,0},{2,3},{3,2},{4,5},{5,4},{6,7},{7,6},{8,9},{9,8},{10,11... | collective-permute-start | bytes 737288 | tf_op jit(solution)/shard_map/ppermute | solution.py:384
  38.4 16.7 %collective-permute-start.1 = (f32[30,16,128]{2,1,0:T(8,128)S(1)}, f32[30,16,128]{2,1,0:T(8,128)S(1)}, u32[]{:S(2)}, u32[]{:S(2)}) collective-permute-start(f32[30,16,128]{2,1,0:T(8,128)S(1)} %get-tuple-element.9), channel_id=1, source_target_pairs={{1,2},{2,1},{3,4},{4,3},{5,6},{6,5},{7,8},{8,7},{9,10},{10,9},{11,... | collective-permute-start | bytes 737288 | tf_op jit(solution)/shard_map/ppermute | solution.py:385

commit v6 on v5

--- a/solution.py
+++ b/solution.py
@@ -397,7 +397,7 @@
         ],
     )
     got = lax.all_to_all(back, "gx", 0, 0)
-    sums = jnp.broadcast_to(jnp.sum(got[:, 6], axis=0), (lines, 8, 128))
+    sums = jnp.broadcast_to(jnp.sum(got[:, 6, 0:4], axis=0), (lines, 4, 128))
     sums = lax.all_to_all(sums, "gy", 0, 0)
     precond, well_update = call(
         unpack_kernel,

time: 84.2 us -> 83.9 us (level)
  no operation moved by 1% of the time
where the time goes in v6:
time: 83.9 us; the launch traced here: 83.6 us
  blocking collectives  72.1 us (86%)
  Pallas kernels  5.54 us (7%)
  starting transfers between devices  5.21 us (6%)
    all_to_all x1, blocking collectives, per_device(): chunks = lax.all_to_all(packed, 'gx', 0, 0)  33.6 us
    all_to_all x1, blocking collectives, per_device(): wells = lax.all_to_all(wells, 'gy', 0, 0, tiled=True)  13.6 us
    all_to_all x1, blocking collectives, per_device(): got = lax.all_to_all(back, 'gx', 0, 0)  12.6 us
    all_to_all x1, blocking collectives, per_device(): sums = lax.all_to_all(sums, 'gy', 0, 0)  12.3 us
    pallas_call x4, Pallas kernels, call(): pl.pallas_call(kernel, out_shape=out_shape, in_specs=[space] * len(inputs...  5.54 us
    ppermute x1, starting transfers between devices, per_device(): lax.ppermute(far, 'gy', [(b, (b + 1 ^ 1) - 1) for b in range(1, lines - 1)])  3.02 us
    ppermute x1, starting transfers between devices, per_device(): near = lax.ppermute(near, 'gy', [(b, b ^ 1) for b in range(lines)])  2.19 us
  transfers between devices with their start and end apart: 2, of which 0 were waited for; matrix products, arithmetic and copies ran while one was open for 0% of the time, Pallas kernels for 0%

profile of v6, /device:TPU:1, one launch (start us, length us, event | category | flops | bytes accessed | tf_op | source)
XLA Modules:
  0.0 83.6 jit_solution(8196649999397960355)
XLA Ops:
  0.6 1.8 %shard_map.95 = f32[8,14,16,128]{3,2,1,0:T(8,128)S(1)} custom-call(f32[6,64,128]{2,1,0:T(8,128)} %bitcast.17, f32[9,64,128]{2,1,0:T(8,128)} %bitcast.16, f32[6,64,128]{2,1,0:T(8,128)} %bitcast.18, f32[6,64,128]{2,1,0:T(8,128)} %bitcast.19, s32[1,64]{1,0:T(1,128)} %bitcast.20, s32[1,64]{1,0:T(1,128)} %bitcast.21, f32[1,64]{1,0:T(1,128)} %bitcast.22, f32[3,4]{1,0:T(4,128)} %wells.1), custom_call_target="tpu_custom_call" | custom-call | tf_op jit(solution)/shard_map/pallas_call | solution.py:331
  2.4 33.6 %all_to_all.26.chunks = f32[8,14,16,128]{3,2,1,0:T(8,128)S(1)} all-to-all(f32[8,14,16,128]{3,2,1,0:T(8,128)S(1)} %shard_map.95), channel_id=1, replica_groups=mesh['gx'=8,'gy'=32] {'gx'}, dimensions={0} | all-to-all | bytes 1835008 | tf_op jit(solution)/shard_map/all_to_all | solution.py:380
  36.0 0.3 shard_map.96
  36.2 2.2 %collective-permute-start = (f32[30,16,128]{2,1,0:T(8,128)S(1)}, f32[30,16,128]{2,1,0:T(8,128)S(1)}, u32[]{:S(2)}, u32[]{:S(2)}) collective-permute-start(f32[30,16,128]{2,1,0:T(8,128)S(1)} %get-tuple-element.8), channel_id=1, source_target_pairs={{0,1},{1,0},{2,3},{3,2},{4,5},{5,4},{6,7},{7,6},{8,9},{9,8},{10,11... | collective-permute-start | bytes 737288 | tf_op jit(solution)/shard_map/ppermute | solution.py:384
  38.4 3.0 %collective-permute-start.1 = (f32[30,16,128]{2,1,0:T(8,128)S(1)}, f32[30,16,128]{2,1,0:T(8,128)S(1)}, u32[]{:S(2)}, u32[]{:S(2)}) collective-permute-start(f32[30,16,128]{2,1,0:T(8,128)S(1)} %get-tuple-element.9), channel_id=1, source_target_pairs={{1,2},{2,1},{3,4},{4,3},{5,6},{6,5},{7,8},{8,7},{9,10},{10,9},{11,... | collective-permute-start | bytes 737288 | tf_op jit(solution)/shard_map/ppermute | solution.py:385
  41.5 13.6 %all_to_all.27 = f32[32,1,128]{2,1,0:T(1,128)S(1)} all-to-all(f32[32,1,128]{2,1,0:T(1,128)S(1)} %bitcast.15), channel_id=1, replica_groups=mesh['gx'=8,'gy'=32] {'gy'}, dimensions={0} | all-to-all | bytes 32768 | tf_op jit(solution)/shard_map/all_to_all | solution.py:387
  55.1 0.0 collective-permute-done.near
  55.1 0.0 collective-permute-done.1.far
  55.1 2.7 %shard_map.97 = f32[8,7,8,128]{3,2,1,0:T(8,128)S(1)} custom-call(f32[8,14,16,128]{3,2,1,0:T(8,128)S(1)} %all_to_all.26.chunks, f32[32,128]{1,0:T(8,128)S(1)} %bitcast.14, f32[30,16,128]{2,1,0:T(8,128)S(1)} %collective-permute-done.near, f32[30,16,128]{2,1,0:T(8,128)S(1)} %collective-permute-done.1.far), custom_call_target="tpu_custom_call" | custom-call | tf_op jit(solution)/shard_map/pallas_call | solution.py:331
  57.8 12.6 %all_to_all.28.chunks = f32[8,7,8,128]{3,2,1,0:T(8,128)S(1)} all-to-all(f32[8,7,8,128]{3,2,1,0:T(8,128)S(1)} %shard_map.97), channel_id=1, replica_groups=mesh['gx'=8,'gy'=32] {'gx'}, dimensions={0} | all-to-all | bytes 458752 | tf_op jit(solution)/shard_map/all_to_all | solution.py:399
  70.4 12.3 %all_to_all.29.sums = f32[32,4,128]{2,1,0:T(4,128)S(1)} all-to-all(f32[32,4,128]{2,1,0:T(4,128)S(1)} %broadcast_in_dim.3), channel_id=1, replica_groups=mesh['gx'=8,'gy'=32] {'gy'}, dimensions={0} | all-to-all | bytes 131072 | tf_op jit(solution)/shard_map/all_to_all | solution.py:401
  82.8 0.8 shard_map.98
  (2 shorter events, 0.0 us)
Async XLA Ops:
  36.2 18.9 %collective-permute-start = (f32[30,16,128]{2,1,0:T(8,128)S(1)}, f32[30,16,128]{2,1,0:T(8,128)S(1)}, u32[]{:S(2)}, u32[]{:S(2)}) collective-permute-start(f32[30,16,128]{2,1,0:T(8,128)S(1)} %get-tuple-element.8), channel_id=1, source_target_pairs={{0,1},{1,0},{2,3},{3,2},{4,5},{5,4},{6,7},{7,6},{8,9},{9,8},{10,11... | collective-permute-start | bytes 737288 | tf_op jit(solution)/shard_map/ppermute | solution.py:384
  38.4 16.7 %collective-permute-start.1 = (f32[30,16,128]{2,1,0:T(8,128)S(1)}, f32[30,16,128]{2,1,0:T(8,128)S(1)}, u32[]{:S(2)}, u32[]{:S(2)}) collective-permute-start(f32[30,16,128]{2,1,0:T(8,128)S(1)} %get-tuple-element.9), channel_id=1, source_target_pairs={{1,2},{2,1},{3,4},{4,3},{5,6},{6,5},{7,8},{8,7},{9,10},{10,9},{11,... | collective-permute-start | bytes 737288 | tf_op jit(solution)/shard_map/ppermute | solution.py:385
